TPU v7x, 32 devices: a whole 2x2x4 slice. The times are simulated.
32 devices in a mesh: rep: 8 (over z, y), shard: 4 (over x, core).
Axes of the slice: x: 2, y: 2, z: 4, core: 2. Of those that a mesh axis runs over, the one named last changes fastest.
Arguments:
- block_input: bfloat16 [8, 1024, 1088], P('rep', 'shard'), may hold values from -6 to 6
- first_gain: bfloat16 [1088], P('shard'), may hold values from 0.5 to 1.5
- first_shift: bfloat16 [1088], P('shard'), may hold values from -4 to 4
- query_key_value_weight: bfloat16 [1088, 3264], P('shard'), may hold values from -0.1875 to 0.1875
- query_bias: bfloat16 [1088], P('shard'), may hold values from -4 to 4
- value_bias: bfloat16 [1088], P('shard'), may hold values from -4 to 4
- attention_output_weight: bfloat16 [1088, 1088], P('shard'), may hold values from -0.75 to 0.75
- attention_output_bias: bfloat16 [1088], P('shard'), may hold values from -4 to 4
- second_gain: bfloat16 [1088], P('shard'), may hold values from 0.5 to 1.5
- second_shift: bfloat16 [1088], P('shard'), may hold values from -4 to 4
- up_weight: bfloat16 [1088, 4352], P('shard'), may hold values from -0.1875 to 0.1875
- up_bias: bfloat16 [4352], P('shard'), may hold values from -6 to 6
- down_weight: bfloat16 [4352, 1088], P('shard'), may hold values from -0.09375 to 0.09375
- down_bias: bfloat16 [1088], P('shard'), may hold values from -4 to 4
- cotangent: float32 [8, 1024, 1088], P('rep', 'shard'), may hold values from -8 to 8
Outputs:
- block_output: float32 [8, 1024, 1088], P('rep', 'shard')
- input_grad: float32 [8, 1024, 1088], P('rep', 'shard')
- first_gain_grad: float32 [1088], P('shard')
- first_shift_grad: float32 [1088], P('shard')
- input_weight_grad: float32 [1088, 3264], P('shard')
- query_bias_grad: float32 [1088], P('shard')
- value_bias_grad: float32 [1088], P('shard')
- output_weight_grad: float32 [1088, 1088], P('shard')
- output_bias_grad: float32 [1088], P('shard')
- second_gain_grad: float32 [1088], P('shard')
- second_shift_grad: float32 [1088], P('shard')
- up_weight_grad: float32 [1088, 4352], P('shard')
- up_bias_grad: float32 [4352], P('shard')
- down_weight_grad: float32 [4352, 1088], P('shard')
- down_bias_grad: float32 [1088], P('shard')
All inputs are finite; a program needn't handle non-finite values.
Results may differ from a plain program's by a relative error of at most 0.017.
Values may be sent and summed in bfloat16 or wider, within the bound.
No kernel may reach another device: no remote copies, remote signals or barrier semaphores. Data moves between devices by JAX's collectives and lax.ppermute only.
A program may use at most 192 MiB of HBM per device.

v0:
```python
import functools

import jax
import jax.numpy as jnp
from jax import lax
from jax.experimental import pallas as pl
from jax.experimental.pallas import tpu as pltpu
from jax.sharding import PartitionSpec as P

HEADS = 17

epsilon = 1e-05
score_scale = 0.125
low = jnp.bfloat16
f32 = jnp.float32


def normalize(values):
    centre = jnp.mean(values, axis=-1, keepdims=True)
    centred = values - centre
    inverse = lax.rsqrt(jnp.mean(centred * centred, axis=-1, keepdims=True) + epsilon)
    return (centred * inverse, inverse)


def norm_back(grad, normed, inverse, gain):
    scaled = grad * gain
    first = jnp.mean(scaled, axis=-1, keepdims=True)
    second = jnp.mean(scaled * normed, axis=-1, keepdims=True)
    return inverse * (scaled - first - normed * second)


def gelu_parts(values):
    cumulative = 0.5 * (1.0 + lax.erf(values * 0.7071067811865476))
    density = jnp.exp(-0.5 * values * values) * 0.3989422804014327
    return values * cumulative, cumulative + values * density


def contract(left, right, left_dim, right_dim):
    return lax.dot_general(
        left, right, (((left_dim,), (right_dim,)), ((), ())), preferred_element_type=f32
    )


def swap(values, bit):
    size = lax.axis_size("shard")
    return lax.ppermute(values, "shard", [(i, i ^ bit) for i in range(size)])


def bits_far_first():
    bit = lax.axis_size("shard") // 2
    bits = []
    while bit:
        bits.append(bit)
        bit //= 2
    return bits


def relative_order():
    order = [0]
    for bit in bits_far_first():
        order = order + [o ^ bit for o in order]
    return order


def gather_relative(block):
    for bit in bits_far_first():
        block = jnp.concatenate([block, swap(block, bit)], axis=0)
    return block


def gather_absolute(block):
    index = lax.axis_index("shard")
    stack = block[None]
    for bit in bits_far_first():
        other = swap(stack, bit)
        upper = (index & bit) != 0
        pair = jnp.stack(
            [jnp.where(upper, other, stack), jnp.where(upper, stack, other)], axis=1
        )
        stack = pair.reshape((2 * stack.shape[0],) + block.shape)
    return stack


def scatter_relative(parts):
    for bit in reversed(bits_far_first()):
        half = parts.shape[0] // 2
        other = swap(parts[half:].astype(low), bit)
        parts = parts[:half] + other.astype(f32)
    return parts


def swap_rep(values, bit):
    size = lax.axis_size("rep")
    return lax.ppermute(values, "rep", [(i, i ^ bit) for i in range(size)])


def rep_bits(turned):
    bits, bit = [], 1
    while bit < lax.axis_size("rep"):
        bits.append(bit)
        bit *= 2
    return bits[1:2] + bits[:1] + bits[2:] if turned else bits


def after(values, gate):
    return lax.optimization_barrier((values, gate))[0]


def half_window(rows):
    return min(rows, (rows + 15) // 16 * 8)


def halve(values, bit):
    rows = values.shape[1]
    window = half_window(rows)
    mine = (lax.axis_index("rep") // bit) % 2
    far = rows - window
    send = lax.dynamic_slice_in_dim(values, (1 - mine) * far, window, 1)
    keep = lax.dynamic_slice_in_dim(values, mine * far, window, 1)
    return keep, swap_rep(send, bit)


def add(keep, other):
    return (keep.astype(f32) + other.astype(f32)).astype(low)


def join(values, other, bit, rows):
    window = values.shape[1]
    upper = (lax.axis_index("rep") // bit) % 2 != 0
    first = jnp.where(upper, other, values)
    second = jnp.where(upper, values, other)
    return jnp.concatenate([first, second[:, 2 * window - rows :]], axis=1)


class Chain:
    def __init__(self, steps):
        self.steps = steps
        self.result = None
        self.take(None)

    def take(self, got):
        try:
            self.waits = self.steps.send(got)
        except StopIteration as end:
            self.waits = None
            self.result = end.value


def advance(chains, gate=()):
    live = [c for c in chains if c.waits is not None]
    arrived, _ = lax.optimization_barrier((tuple(c.waits for c in live), gate))
    for chain, got in zip(live, arrived):
        chain.take(got)


def scatter_steps(lanes, orders):
    sizes = []
    for step in range(len(orders[0])):
        sizes.append(lanes[0].shape[1])
        halves = [halve(v, order[step]) for v, order in zip(lanes, orders)]
        others = yield tuple(h[1] for h in halves)
        lanes = [add(h[0], other) for h, other in zip(halves, others)]
    return list(lax.optimization_barrier(tuple(lanes))), sizes


def gather_steps(lanes, orders, sizes):
    for step in reversed(range(len(orders[0]))):
        others = yield tuple(swap_rep(v, order[step]) for v, order in zip(lanes, orders))
        lanes = [
            join(v, other, order[step], sizes[step])
            for v, other, order in zip(lanes, others, orders)
        ]
    return lanes


def exchange_steps(blocks):
    size = lax.axis_size("shard")
    index = lax.axis_index("shard")
    pieces = [lax.dynamic_index_in_dim(blocks, index ^ o, 0, keepdims=True) for o in range(size)]
    others = yield tuple(swap(pieces[o], o) for o in range(1, size))
    result = jnp.zeros_like(blocks)
    for o, piece in enumerate(pieces[:1] + list(others)):
        result = lax.dynamic_update_slice_in_dim(result, piece, index ^ o, 0)
    return [result[i] for i in range(size)]


def plain_sum(values, order):
    lanes, sizes = yield from scatter_steps([values], [order])
    lanes = yield from gather_steps(lanes, [order], sizes)
    return lanes[0]


def turned_sum(values, order):
    lanes, sizes = yield from scatter_steps([values], [order])
    blocks = yield from exchange_steps(lanes[0])
    lanes = yield from gather_steps([jnp.concatenate(blocks, axis=1)[None]], [order], sizes)
    return lanes[0][0]


def mixer_sum(first, second, orders, own):
    lanes, sizes = yield from scatter_steps([first, second], orders)
    blocks = yield from exchange_steps(
        jnp.concatenate([lanes[0], lanes[1][:, :, :own]], axis=2)
    )
    parts = [
        jnp.concatenate([b[:, i * own : (i + 1) * own] for b in blocks], axis=1) for i in range(3)
    ]
    output = jnp.concatenate([lanes[1][i, :, own:] for i in range(len(blocks))], axis=1)
    lanes = [
        jnp.concatenate(parts[:2], axis=1)[None],
        jnp.concatenate([parts[2], output], axis=1)[None],
    ]
    lanes = yield from gather_steps(lanes, orders, sizes)
    return lanes[0][0], lanes[1][0]


def shard_sum(parts):
    for bit in reversed(bits_far_first()):
        half = parts.shape[0] // 2
        (other,) = yield (swap(parts[half:].astype(low), bit),)
        parts = parts[:half] + other.astype(f32)
    return parts


def vector_sum(partial, complete, own_part):
    for bit in bits_far_first():
        (other,) = yield (swap(partial, bit),)
        partial = partial + other
    total = jnp.concatenate([own_part(p) for p in partial] + complete)
    for bit in rep_bits(False):
        (other,) = yield (swap_rep(total, bit),)
        total = total + other
    return total


def exchange(blocks):
    size = lax.axis_size("shard")
    index = lax.axis_index("shard")
    result = jnp.zeros_like(blocks)
    for offset in range(size):
        peer = index ^ offset
        piece = lax.dynamic_index_in_dim(blocks, peer, 0, keepdims=True)
        if offset:
            piece = swap(piece, offset)
        result = lax.dynamic_update_slice_in_dim(result, piece, peer, 0)
    return result


def send_halves(blocks):
    index = lax.axis_index("shard")
    size = lax.axis_size("shard")
    half = blocks.shape[1] // 2
    part = (lax.axis_index("rep") % 2) * half
    pieces = []
    for offset in range(size):
        piece = lax.dynamic_index_in_dim(blocks, index ^ offset, 0, keepdims=True)
        if offset >= 2:
            piece = lax.dynamic_slice_in_dim(piece, part, half, 1)
        if offset:
            piece = swap(piece, offset)
        pieces.append(piece)
    return pieces


def join_halves(pieces):
    index = lax.axis_index("shard")
    upper = lax.axis_index("rep") % 2 != 0
    full = pieces[0].shape[1]
    count = len(pieces)
    if count > 2:
        mine = jnp.concatenate(pieces[2:], axis=0)
        other = swap_rep(mine, 1)
        halves = jnp.concatenate(
            [jnp.where(upper, other, mine), jnp.where(upper, mine, other)], axis=1
        )
        pieces = pieces[:2] + [halves[i : i + 1] for i in range(count - 2)]
    result = jnp.zeros((count,) + pieces[0].shape[1:], pieces[0].dtype)
    for offset, piece in enumerate(pieces):
        result = lax.dynamic_update_slice_in_dim(result, piece, index ^ offset, 0)
    return result


def visible_part(scores, top, block, fill):
    rows = lax.broadcasted_iota(jnp.int32, (block, block), 0)
    cols = lax.broadcasted_iota(jnp.int32, (block, block), 1)
    last = jnp.where(rows <= cols, scores[top:], fill)
    if top == 0:
        return last
    return jnp.concatenate([scores[:top], last], axis=0)


def turn(values):
    return values.astype(f32).T


def forward_kernel(blocks, block, place, q_ref, k_ref, v_ref, o_ref, low_ref, log_ref, k_rows, v_cols):
    for i in range(blocks):
        here = pl.ds(pl.multiple_of(place[i] * block, block), block)
        there = pl.ds(i * block, block)
        k_rows[there, :] = turn(k_ref[:, here]).astype(low)
        v_cols[:, there] = v_ref[:, here]
    for i in range(blocks):
        here = pl.ds(pl.multiple_of(place[i] * block, block), block)
        top = i * block
        count = top + block
        q_cols = q_ref[:, here] * jnp.asarray(score_scale, low)
        scores = contract(k_rows[:count, :], q_cols, 1, 0)
        scores = visible_part(scores, top, block, -jnp.inf)
        peak = jnp.max(scores, axis=0, keepdims=True)
        weights = jnp.exp(scores - peak)
        total = jnp.sum(weights, axis=0, keepdims=True)
        mixed = contract(v_cols[:, :count], weights.astype(low), 1, 0) / total
        o_ref[:, here] = mixed
        low_ref[:, here] = mixed.astype(low)
        log_ref[0, :, here] = peak + jnp.log(total)


def backward_kernel(
    blocks,
    block,
    place,
    q_ref,
    k_ref,
    v_ref,
    g_ref,
    o_ref,
    log_ref,
    dq_ref,
    dk_ref,
    dv_ref,
    k_rows,
    v_rows,
    k_cols,
    dk_rows,
    dv_rows,
):
    for i in range(blocks):
        here = pl.ds(pl.multiple_of(place[i] * block, block), block)
        there = pl.ds(i * block, block)
        k_rows[there, :] = turn(k_ref[:, here]).astype(low)
        v_rows[there, :] = turn(v_ref[:, here]).astype(low)
        k_cols[:, there] = k_ref[:, here]
    for i in reversed(range(blocks)):
        here = pl.ds(pl.multiple_of(place[i] * block, block), block)
        top = i * block
        count = top + block
        q_cols = q_ref[:, here] * jnp.asarray(score_scale, low)
        g_cols = g_ref[:, here]
        q_rows = turn(q_cols).astype(low)
        g_rows = turn(g_cols).astype(low)
        correction = jnp.sum(g_cols.astype(f32) * o_ref[:, here], axis=0, keepdims=True)
        scores = contract(k_rows[:count, :], q_cols, 1, 0)
        probs = jnp.exp(scores - log_ref[0, :, here])
        probs = visible_part(probs, top, block, 0.0)
        grad_probs = contract(v_rows[:count, :], g_cols, 1, 0)
        grad_scores = (probs * (grad_probs - correction)).astype(low)
        dv_part = contract(probs.astype(low), g_rows, 1, 0)
        dk_part = contract(grad_scores, q_rows, 1, 0)
        if i == blocks - 1:
            dv_rows[:count, :] = dv_part
            dk_rows[:count, :] = dk_part
        else:
            dv_rows[:count, :] += dv_part
            dk_rows[:count, :] += dk_part
        dq = contract(k_cols[:, :count], grad_scores, 1, 0) * score_scale
        dq_ref[:, here] = dq.astype(low)
    for i in range(blocks):
        here = pl.ds(pl.multiple_of(place[i] * block, block), block)
        there = pl.ds(i * block, block)
        dk_ref[:, here] = dk_rows[there, :].T.astype(low)
        dv_ref[:, here] = dv_rows[there, :].T.astype(low)


def head_spec(size, length, first):
    return pl.BlockSpec((size, length), lambda h, place: (first + h, 0))


def attend_forward(place, projected, heads, block):
    size = projected.shape[0] // (3 * heads)
    length = projected.shape[1]
    blocks = length // block
    row = pl.BlockSpec((1, 1, length), lambda h, place: (h, 0, 0))
    return pl.pallas_call(
        functools.partial(forward_kernel, blocks, block),
        grid_spec=pltpu.PrefetchScalarGridSpec(
            num_scalar_prefetch=1,
            grid=(heads,),
            in_specs=[
                head_spec(size, length, 0),
                head_spec(size, length, heads),
                head_spec(size, length, 2 * heads),
            ],
            out_specs=[head_spec(size, length, 0), head_spec(size, length, 0), row],
            scratch_shapes=[
                pltpu.VMEM((length, size), low),
                pltpu.VMEM((size, length), low),
            ],
        ),
        out_shape=[
            jax.ShapeDtypeStruct((heads * size, length), f32),
            jax.ShapeDtypeStruct((heads * size, length), low),
            jax.ShapeDtypeStruct((heads, 1, length), f32),
        ],
        cost_estimate=pl.CostEstimate(
            flops=4 * heads * length * length * size,
            bytes_accessed=heads * length * size * 12,
            transcendentals=heads * length * length,
        ),
        compiler_params=pltpu.CompilerParams(vmem_limit_bytes=32 * 1024 * 1024),
        name="attend_forward",
    )(place, projected, projected, projected)


def attend_backward(place, projected, grad, mixed, log_total, heads, block):
    size = projected.shape[0] // (3 * heads)
    length = projected.shape[1]
    blocks = length // block
    row = pl.BlockSpec((1, 1, length), lambda h, place: (h, 0, 0))
    out = jax.ShapeDtypeStruct((heads * size, length), low)
    return pl.pallas_call(
        functools.partial(backward_kernel, blocks, block),
        grid_spec=pltpu.PrefetchScalarGridSpec(
            num_scalar_prefetch=1,
            grid=(heads,),
            in_specs=[
                head_spec(size, length, 0),
                head_spec(size, length, heads),
                head_spec(size, length, 2 * heads),
                head_spec(size, length, 0),
                head_spec(size, length, 0),
                row,
            ],
            out_specs=[head_spec(size, length, 0)] * 3,
            scratch_shapes=[
                pltpu.VMEM((length, size), low),
                pltpu.VMEM((length, size), low),
                pltpu.VMEM((size, length), low),
                pltpu.VMEM((length, size), f32),
                pltpu.VMEM((length, size), f32),
            ],
        ),
        out_shape=[out, out, out],
        cost_estimate=pl.CostEstimate(
            flops=10 * heads * length * length * size,
            bytes_accessed=heads * length * size * 20,
            transcendentals=heads * length * length,
        ),
        compiler_params=pltpu.CompilerParams(vmem_limit_bytes=32 * 1024 * 1024),
        name="attend_backward",
    )(place, projected, projected, projected, grad, mixed, log_total)


def local(
    block_input,
    first_gain,
    first_shift,
    query_key_value_weight,
    query_bias,
    value_bias,
    attention_output_weight,
    attention_output_bias,
    second_gain,
    second_shift,
    up_weight,
    up_bias,
    down_weight,
    down_bias,
    cotangent,
):
    shards = lax.axis_size("shard")
    index = lax.axis_index("shard")
    seqs, span, width = block_input.shape
    size = width // HEADS
    own = width // shards
    hidden = up_bias.shape[0]
    starts = [d * own // size for d in range(shards)]
    heads = max(-(-(d + 1) * own // size) - starts[d] for d in range(shards))
    window = heads * size
    pad = window - own
    start = index * own // size
    skew = index * own - start * size
    order = relative_order()
    inverse_order = jnp.asarray([order.index(o) for o in range(shards)], jnp.int32)
    place = inverse_order[jnp.arange(shards, dtype=jnp.int32) ^ index]

    own_input = block_input.reshape(seqs * span, width)
    inputs_all = gather_relative(own_input)
    vectors = gather_absolute(
        jnp.stack(
            [
                first_gain,
                first_shift,
                query_bias,
                value_bias,
                attention_output_bias,
                second_gain,
                second_shift,
                down_bias,
            ]
        )
    )
    vectors = vectors.transpose(1, 0, 2).reshape(8, width)
    gain_one, shift_one, bias_query, bias_value, bias_out, gain_two, shift_two, bias_down = (
        vectors[i] for i in range(8)
    )
    weight_in = exchange(
        jnp.stack(
            [
                jnp.concatenate(
                    [
                        query_key_value_weight[
                            :, part * width + s * size : part * width + s * size + window
                        ]
                        for part in range(3)
                    ],
                    axis=1,
                )
                for s in starts
            ]
        )
    ).reshape(width, 3 * window)
    up_blocks = jnp.stack([up_weight[:, s * hidden : (s + 1) * hidden] for s in range(shards)])
    up_pieces = send_halves(after(up_blocks, weight_in))
    to_right = [(i, i + 1) for i in range(shards - 1)]
    to_left = [(i + 1, i) for i in range(shards - 1)]
    weight_out_window = lax.dynamic_slice_in_dim(
        jnp.concatenate(
            [
                lax.ppermute(attention_output_weight[own - pad :], "shard", to_right),
                attention_output_weight,
                lax.ppermute(attention_output_weight[:pad], "shard", to_left),
            ],
            axis=0,
        ),
        pad - skew,
        window,
        0,
    )
    branch = gather_relative(after(cotangent.reshape(seqs * span, width).astype(low), up_pieces))
    grad_out = cotangent.reshape(seqs * span, width)

    def own_rows(values):
        return lax.dynamic_slice_in_dim(values, skew, own, 0)

    rows = shards * seqs * span
    normed_all, _ = normalize(inputs_all.astype(f32))
    hidden_one = (normed_all * gain_one + shift_one).astype(low)
    bias_window = jnp.concatenate(
        [
            lax.dynamic_slice_in_dim(bias_query, start * size, window, 0),
            jnp.zeros((window,), low),
            lax.dynamic_slice_in_dim(bias_value, start * size, window, 0),
        ]
    ).astype(f32)
    projected = (contract(weight_in, hidden_one, 0, 1) + bias_window[:, None]).astype(low)

    def per_sequence(values):
        lead = values.shape[:-1]
        split = values.reshape(lead + (shards, seqs, span))
        return [split[..., :, s, :].reshape(lead + (shards * span,)) for s in range(seqs)]

    def join_sequences(parts):
        if seqs == 1:
            return parts[0]
        lead = parts[0].shape[:-1]
        joined = jnp.stack([p.reshape(lead + (shards, span)) for p in parts], axis=-2)
        return joined.reshape(lead + (rows,))

    projected_parts = per_sequence(projected) if seqs > 1 else [projected]
    forward_parts = [attend_forward(place, p, heads, span) for p in projected_parts]
    attended = join_sequences([p[1] for p in forward_parts])
    attended, up_pieces = lax.optimization_barrier((attended, up_pieces))
    attended = own_rows(attended)
    weight_up = join_halves(up_pieces).reshape(width, hidden)
    mixed_sum = scatter_relative(
        contract(attended, attention_output_weight, 0, 0)
    )
    layer_input = own_input.astype(f32)
    middle = layer_input + mixed_sum + bias_out

    normed_two, inverse_two = normalize(middle)
    hidden_two = gather_relative((normed_two * gain_two + shift_two).astype(low))
    before = contract(hidden_two, weight_up, 1, 0) + up_bias
    activated, slope = gelu_parts(before)
    activated = activated.astype(low)
    grad_before = (contract(branch, down_weight, 1, 1) * slope).astype(low)
    hidden_two_sum = contract(grad_before, weight_up, 1, 1)
    hidden_two_sum, late_before, late_active = lax.optimization_barrier(
        (hidden_two_sum, grad_before, activated)
    )
    grad_hidden_two = scatter_relative(hidden_two_sum)
    down_weight_grad = contract(late_active, branch, 0, 0).astype(low)[None]
    up_weight_grad = contract(hidden_two, late_before, 0, 0).astype(low)
    up_weight_grad = up_weight_grad.reshape(shards, own, hidden)
    down_sum = contract(late_active, down_weight, 1, 0)
    grad_middle = grad_out + norm_back(grad_hidden_two, normed_two, inverse_two, gain_two)
    near, far = rep_bits(False), rep_bits(True)
    down_chain = Chain(plain_sum(down_weight_grad, near))
    up_chain = Chain(turned_sum(up_weight_grad, far))
    advance([down_chain, up_chain], grad_middle)

    grad_mixed = gather_relative(grad_middle.astype(low))
    grad_attended = contract(weight_out_window, grad_mixed, 1, 1).astype(low)
    grad_parts = per_sequence(grad_attended) if seqs > 1 else [grad_attended]
    backward_parts = [
        attend_backward(place, p, g, f[0], f[2], heads, span)
        for p, g, f in zip(projected_parts, grad_parts, forward_parts)
    ]
    grad_query, grad_key, grad_value = (
        join_sequences([p[i] for p in backward_parts]) for i in range(3)
    )
    own_query, own_key, own_value = (own_rows(g) for g in (grad_query, grad_key, grad_value))
    own_projected = jnp.concatenate([own_query, own_key, own_value], axis=0)
    line = jnp.arange(window)
    mine = ((line >= skew) & (line < skew + own))[:, None]
    grad_projected = jnp.concatenate(
        [jnp.where(mine, g, jnp.zeros_like(g)) for g in (grad_query, grad_key, grad_value)], axis=0
    )
    output_weight_grad = contract(attended, grad_mixed, 1, 0).astype(low)
    block_chain = Chain(shard_sum(after(down_sum, grad_mixed)))
    advance([down_chain, up_chain, block_chain], grad_query)

    def by_owner(gradient):
        return gradient.reshape(shards, own, gradient.shape[1])

    first_part = by_owner(contract(hidden_one, own_projected[: 2 * own], 0, 1).astype(low))
    second_part = by_owner(contract(hidden_one, own_value, 0, 1).astype(low))
    output_blocks = jnp.stack(
        [output_weight_grad[:, s * own : (s + 1) * own] for s in range(shards)]
    )
    second_part = jnp.concatenate([second_part, output_blocks], axis=2)
    mixer_chain = Chain(mixer_sum(first_part, second_part, [near, far], own))
    hidden_chain = Chain(shard_sum(contract(grad_projected, weight_in, 0, 1)))
    chains = [down_chain, up_chain, block_chain, mixer_chain, hidden_chain]
    while hidden_chain.waits is not None:
        advance(chains)
    block_output = middle + block_chain.result + bias_down
    grad_hidden_one = hidden_chain.result
    normed_one, inverse_one = normalize(layer_input)
    input_grad = grad_middle + norm_back(grad_hidden_one, normed_one, inverse_one, gain_one)

    def own_part(values):
        return lax.dynamic_slice_in_dim(values, index * own, own, 0)

    partial = jnp.stack(
        [
            jnp.sum(grad_hidden_one * normed_one, axis=0),
            jnp.sum(grad_hidden_one, axis=0),
            jnp.sum(grad_hidden_two * normed_two, axis=0),
            jnp.sum(grad_hidden_two, axis=0),
        ]
    )
    vector_chain = Chain(
        vector_sum(
            partial,
            [
                jnp.sum(own_query.astype(f32), axis=1),
                jnp.sum(own_value.astype(f32), axis=1),
                own_part(jnp.sum(grad_mixed.astype(f32), axis=0)),
                own_part(jnp.sum(branch.astype(f32), axis=0)),
                jnp.sum(grad_before.astype(f32), axis=0),
            ],
            own_part,
        )
    )
    chains.append(vector_chain)
    while any(c.waits is not None for c in chains):
        advance(chains)
    complete = vector_chain.result
    down_weight_grad = down_chain.result[0]
    up_weight_grad = up_chain.result
    first_part, second_part = mixer_chain.result
    input_weight_grad = jnp.concatenate([first_part, second_part[:, :width]], axis=1)
    output_weight_grad = second_part[:, width:]
    (
        first_gain_grad,
        first_shift_grad,
        second_gain_grad,
        second_shift_grad,
        query_bias_grad,
        value_bias_grad,
        output_bias_grad,
        down_bias_grad,
    ) = (complete[i * own : (i + 1) * own] for i in range(8))
    up_bias_grad = complete[8 * own :]
    return (
        block_output.reshape(seqs, span, width),
        input_grad.reshape(seqs, span, width),
        first_gain_grad,
        first_shift_grad,
        input_weight_grad.astype(f32),
        query_bias_grad,
        value_bias_grad,
        output_weight_grad.astype(f32),
        output_bias_grad,
        second_gain_grad,
        second_shift_grad,
        up_weight_grad.astype(f32),
        up_bias_grad,
        down_weight_grad.astype(f32),
        down_bias_grad,
    )


def solution(mesh):
    matrix, vector, tokens = P("shard", None), P("shard"), P("rep", "shard", None)
    return jax.shard_map(
        local,
        mesh=mesh,
        in_specs=(
            tokens,
            vector,
            vector,
            matrix,
            vector,
            vector,
            matrix,
            vector,
            vector,
            vector,
            matrix,
            vector,
            matrix,
            vector,
            tokens,
        ),
        out_specs=(
            tokens,
            tokens,
            vector,
            vector,
            matrix,
            vector,
            vector,
            matrix,
            vector,
            vector,
            vector,
            matrix,
            vector,
            matrix,
            vector,
        ),
        check_vma=False,
    )
```

profile of v0, /device:TPU:0, one launch (start us, length us, event | category | flops | bytes accessed | tf_op | source)
XLA Modules:
  0.0 458.6 jit_solution(8082880222089648596)
XLA Ops:
  6.9 2.9 collective-permute-start.5
  9.9 3.2 fusion.87
  30.3 17.9 %collective-permute-done.1 = bf16[1,272,960]{2,1,0:T(8,128)(2,1)} collective-permute-done((bf16[1,272,960]{2,1,0:T(8,128)(2,1)}, bf16[1,272,960]{2,1,0:T(8,128)(2,1)}, u32[]{:S(2)}, u32[]{:S(2)}) %collective-permute-start.1) | collective-permute-done | bytes 522272 | tf_op jit(solution)/shard_map/ppermute | solution.py:46
  58.8 2.3 fusion.5
  62.5 2.8 add_convert_fusion.q_ref.k_ref.v_ref
  65.4 10.5 %attend_forward.1 = (f32[320,1024]{1,0:T(8,128)S(1)}, bf16[320,1024]{1,0:T(8,128)(2,1)S(1)}, f32[5,1,1024]{2,1,0:T(1,128)S(1)}) custom-call(s32[4]{0:T(128)S(1)} %gather_fusion, bf16[960,1024]{1,0:T(8,128)(2,1)S(1)} %add_convert_fusion.q_ref.k_ref.v_ref, bf16[960,1024]{1,0:T(8,128)(2,1)S(1)} %add_convert_fusion.q_ref.k_ref.v_ref, ...), custom_call_target="tpu_custom_call" | custom-call | flops 1342177280 | bytes 3932160 | tf_op jit(solution)/shard_map/attend_forward/pallas_call | solution.py:383
  82.7 2.3 slice_add_fusion.1
  86.8 10.0 %collective-permute-done.12 = bf16[256,1088]{0,1:T(8,128)(2,1)S(1)} collective-permute-done((bf16[256,1088]{0,1:T(8,128)(2,1)}, bf16[256,1088]{0,1:T(8,128)(2,1)S(1)}, u32[]{:S(2)}, u32[]{:S(2)}) %collective-permute-start.12) | collective-permute-done | bytes 557088 | tf_op jit(solution)/shard_map/ppermute | solution.py:46
  98.7 9.1 %collective-permute-done.11 = bf16[256,1088]{0,1:T(8,128)(2,1)S(1)} collective-permute-done((bf16[256,1088]{0,1:T(8,128)(2,1)S(1)}, bf16[256,1088]{0,1:T(8,128)(2,1)S(1)}, u32[]{:S(2)}, u32[]{:S(2)}) %collective-permute-start.11) | collective-permute-done | bytes 557088 | tf_op jit(solution)/shard_map/ppermute | solution.py:46
  111.5 12.4 %collective-permute-done.14 = bf16[256,1088]{0,1:T(8,128)(2,1)S(1)} collective-permute-done((bf16[256,1088]{0,1:T(8,128)(2,1)S(1)}, bf16[256,1088]{0,1:T(8,128)(2,1)S(1)}, u32[]{:S(2)}, u32[]{:S(2)}) %collective-permute-start.14) | collective-permute-done | bytes 557088 | tf_op jit(solution)/shard_map/ppermute | solution.py:46
  126.8 5.1 %multiply_convert_fusion = (bf16[1024,1088]{0,1:T(8,128)(2,1)}, f32[1024,1088]{0,1:T(8,128)S(1)}) fusion(f32[1088]{0:T(1024)S(1)} %convert_element_type.312, bf16[1088,1088]{1,0:T(8,128)(2,1)S(1)} %bitcast.148, bf16[512,1088]{0,1:T(8,128)(2,1)S(1)} %collective-permute-done.15, bf16[256,1088]{0,1:T(8,128)(2,1)S(1)} %collective-permute-done.14, ...), kind=kOutput, calls=%fused_computation.21 | convolution fusion | flops 2437677056 | bytes 11284736 | tf_op jit(solution)/shard_map/dot_general | solution.py:39
  131.9 5.3 %convert_reduce_fusion.1 = (f32[1088]{0:T(1024)}, bf16[1024,1088]{0,1:T(8,128)(2,1)S(1)}) fusion(f32[1024,1088]{0,1:T(8,128)S(1)} %get-tuple-element.254, bf16[1088,1088]{1,0:T(8,128)(2,1)S(1)} %copy-done, bf16[1024,1088]{0,1:T(8,128)(2,1)S(1)} %constant_dynamic-update-slice_fusion.13), kind=kOutput, calls=%fused_computation.18 | convolution fusion | flops 2437676032 | bytes 11284736 | tf_op jit(solution)/shard_map/dot_general | solution.py:39
  137.2 3.1 fusion.96
  146.6 13.9 %collective-permute-start.26 = (bf16[48,1088]{1,0:T(8,128)(2,1)S(1)}, bf16[48,1088]{1,0:T(8,128)(2,1)}, u32[]{:S(2)}, u32[]{:S(2)}) collective-permute-start(bf16[48,1088]{1,0:T(8,128)(2,1)S(1)} %get-tuple-element.200), channel_id=1, source_target_pairs={{0,1},{1,2},{2,3},{4,5},{5,6},{6,7},{8,9},{9,10},{10,11},{12,13},{... | collective-permute-start | bytes 313352 | tf_op jit(solution)/shard_map/ppermute | solution.py:529
  161.9 5.4 %convolution_convert_fusion.1 = bf16[1088,1088]{1,0:T(8,128)(2,1)S(1)} fusion(bf16[1024,1088]{0,1:T(8,128)(2,1)} %get-tuple-element.81, bf16[1024,1088]{0,1:T(8,128)(2,1)} %copy-done.26), kind=kOutput, calls=%fused_computation.2 | convolution fusion | flops 2425491456 | bytes 6823936 | tf_op jit(solution)/shard_map/dot_general | solution.py:39
  169.0 2.3 convert_add_fusion.2
  172.7 3.3 convolution_convert_fusion
  177.8 9.2 %collective-permute-done.18 = bf16[256,1088]{0,1:T(8,128)(2,1)S(1)} collective-permute-done((bf16[256,1088]{0,1:T(8,128)(2,1)S(1)}, bf16[256,1088]{0,1:T(8,128)(2,1)S(1)}, u32[]{:S(2)}, u32[]{:S(2)}) %collective-permute-start.18) | collective-permute-done | bytes 557088 | tf_op jit(solution)/shard_map/ppermute | solution.py:46
  190.3 4.7 %fusion.95 = f32[1024,1088]{0,1:T(8,128)} fusion(bf16[1024,1088]{0,1:T(8,128)(2,1)S(1)} %copy-done.71, bf16[1088,1088]{1,0:T(8,128)(2,1)S(1)} %copy-done), kind=kOutput, calls=%fused_computation.323 | convolution fusion | flops 2424307712 | bytes 9052160 | tf_op jit(solution)/shard_map/dot_general | solution.py:39
  195.1 2.6 collective-permute-done.21
  197.7 7.8 %collective-permute-done.22 = bf16[4,136,1088]{2,1,0:T(8,128)(2,1)S(1)} collective-permute-done((bf16[4,136,1088]{2,1,0:T(8,128)(2,1)S(1)}, bf16[4,136,1088]{2,1,0:T(8,128)(2,1)S(1)}, u32[]{:S(2)}, u32[]{:S(2)}) %collective-permute-start.22) | collective-permute-done | bytes 1183776 | tf_op jit(solution)/shard_map/ppermute | solution.py:94
  215.6 10.6 %attend_backward.1 = (bf16[320,1024]{1,0:T(8,128)(2,1)S(1)}, bf16[320,1024]{1,0:T(8,128)(2,1)S(1)}, bf16[320,1024]{1,0:T(8,128)(2,1)S(1)}) custom-call(s32[4]{0:T(128)S(1)} %gather_fusion, bf16[960,1024]{1,0:T(8,128)(2,1)S(1)} %copy-done.3, bf16[960,1024]{1,0:T(8,128)(2,1)S(1)} %copy-done.3, bf16[960,1024]{1,0:T(8,128)(2,1)S(1)} %copy-done.3, ...), custom_call_target="tpu_custom_call" | custom-call | flops 3355443200 | bytes 6553600 | tf_op jit(solution)/shard_map/attend_backward/pallas_call | solution.py:420
  229.6 2.7 convolution_convert_fusion.2
  232.3 2.7 copy.35
  241.5 2.5 fusion.14
  246.9 2.7 collective-permute-start.28
  252.7 11.0 %collective-permute-done.32 = bf16[4,136,544]{2,1,0:T(8,128)(2,1)S(1)} collective-permute-done((bf16[4,136,544]{2,1,0:T(8,128)(2,1)S(1)}, bf16[4,136,544]{2,1,0:T(8,128)(2,1)S(1)}, u32[]{:S(2)}, u32[]{:S(2)}) %collective-permute-start.32) | collective-permute-done | bytes 591904 | tf_op jit(solution)/shard_map/ppermute | solution.py:94
  265.1 16.6 %collective-permute-done.29 = bf16[4,40,1088]{2,1,0:T(8,128)(2,1)S(1)} collective-permute-done((bf16[4,40,1088]{2,1,0:T(8,128)(2,1)S(1)}, bf16[4,40,1088]{2,1,0:T(8,128)(2,1)S(1)}, u32[]{:S(2)}, u32[]{:S(2)}) %collective-permute-start.29) | collective-permute-done | bytes 348192 | tf_op jit(solution)/shard_map/ppermute | solution.py:94
  292.5 9.1 %collective-permute-done.34 = bf16[1,136,1088]{2,1,0:T(8,128)(2,1)S(1)} collective-permute-done((bf16[1,136,1088]{2,1,0:T(8,128)(2,1)S(1)}, bf16[1,136,1088]{2,1,0:T(8,128)(2,1)S(1)}, u32[]{:S(2)}, u32[]{:S(2)}) %collective-permute-start.34) | collective-permute-done | bytes 295968 | tf_op jit(solution)/shard_map/ppermute | solution.py:94
  301.6 3.4 collective-permute-done.38
  310.6 2.6 collective-permute-start.43
  315.9 2.5 collective-permute-start.41
  318.4 2.7 fusion.29
  321.1 12.5 %collective-permute-done.44 = bf16[4,40,544]{2,1,0:T(8,128)(2,1)} collective-permute-done((bf16[4,40,544]{2,1,0:T(8,128)(2,1)}, bf16[4,40,544]{2,1,0:T(8,128)(2,1)}, u32[]{:S(2)}, u32[]{:S(2)}) %collective-permute-start.44) | collective-permute-done | bytes 174112 | tf_op jit(solution)/shard_map/ppermute | solution.py:94
  333.6 4.4 collective-permute-done.43
  338.0 7.3 %collective-permute-done.42 = bf16[1,40,4352]{2,1,0:T(8,128)(2,1)S(1)} collective-permute-done((bf16[1,40,4352]{2,1,0:T(8,128)(2,1)S(1)}, bf16[1,40,4352]{2,1,0:T(8,128)(2,1)S(1)}, u32[]{:S(2)}, u32[]{:S(2)}) %collective-permute-start.42) | collective-permute-done | bytes 348192 | tf_op jit(solution)/shard_map/ppermute | solution.py:94
  354.2 3.5 collective-permute-done.49
  357.7 32.9 %collective-permute-done.47 = bf16[1,72,4352]{2,1,0:T(8,128)(2,1)S(1)} collective-permute-done((bf16[1,72,4352]{2,1,0:T(8,128)(2,1)S(1)}, bf16[1,72,4352]{2,1,0:T(8,128)(2,1)S(1)}, u32[]{:S(2)}, u32[]{:S(2)}) %collective-permute-start.47) | collective-permute-done | bytes 626720 | tf_op jit(solution)/shard_map/ppermute | solution.py:94
  394.1 3.0 collective-permute-start.54
  399.0 2.6 fusion.11
  401.6 4.3 collective-permute-done.53
  405.9 2.6 collective-permute-done.54
  408.5 20.4 %collective-permute-done.52 = bf16[1,136,4352]{2,1,0:T(8,128)(2,1)S(1)} collective-permute-done((bf16[1,136,4352]{2,1,0:T(8,128)(2,1)S(1)}, bf16[1,136,4352]{2,1,0:T(8,128)(2,1)S(1)}, u32[]{:S(2)}, u32[]{:S(2)}) %collective-permute-start.52) | collective-permute-done | bytes 1183776 | tf_op jit(solution)/shard_map/ppermute | solution.py:94
  432.8 3.4 collective-permute-done.56
  436.2 4.6 %collective-permute-done.57 = bf16[1,72,2176]{2,1,0:T(8,128)(2,1)S(1)} collective-permute-done((bf16[1,72,2176]{2,1,0:T(8,128)(2,1)S(1)}, bf16[1,72,2176]{2,1,0:T(8,128)(2,1)S(1)}, u32[]{:S(2)}, u32[]{:S(2)}) %collective-permute-start.57) | collective-permute-done | bytes 313376 | tf_op jit(solution)/shard_map/ppermute | solution.py:94
  441.5 2.5 collective-permute-start.60
  444.0 2.5 fusion.13
  446.5 4.7 %collective-permute-done.59 = bf16[1,136,2176]{2,1,0:T(8,128)(2,1)S(1)} collective-permute-done((bf16[1,136,2176]{2,1,0:T(8,128)(2,1)S(1)}, bf16[1,136,2176]{2,1,0:T(8,128)(2,1)S(1)}, u32[]{:S(2)}, u32[]{:S(2)}) %collective-permute-start.59) | collective-permute-done | bytes 591904 | tf_op jit(solution)/shard_map/ppermute | solution.py:94
  (443 shorter events, 139.1 us)
Async XLA Ops:
  6.9 14.9 %collective-permute-start.5 = (bf16[1,8,272]{2,1,0:T(8,128)(2,1)}, bf16[1,8,272]{2,1,0:T(8,128)(2,1)}, u32[]{:S(2)}, u32[]{:S(2)}) collective-permute-start(bf16[1,8,272]{2,1,0:T(8,128)(2,1)} %bitcast.7), channel_id=1, source_target_pairs={{0,2},{1,3},{2,0},{3,1},{4,6},{5,7},{6,4},{7,5},{8,10},{9,11},{10,... | collective-permute-start | bytes 13064 | tf_op jit(solution)/shard_map/ppermute | solution.py:46
  9.8 15.9 %collective-permute-start.3 = (bf16[256,1088]{0,1:T(8,128)(2,1)}, bf16[256,1088]{0,1:T(8,128)(2,1)}, u32[]{:S(2)}, u32[]{:S(2)}) collective-permute-start(bf16[256,1088]{0,1:T(8,128)(2,1)} %bitcast.136), channel_id=1, source_target_pairs={{0,2},{1,3},{2,0},{3,1},{4,6},{5,7},{6,4},{7,5},{8,10},{9,11},{10,... | collective-permute-start | bytes 1671176 | tf_op jit(solution)/shard_map/ppermute | solution.py:46
  17.0 33.0 %collective-permute-start.2 = (bf16[1,272,960]{2,1,0:T(8,128)(2,1)}, bf16[1,272,960]{2,1,0:T(8,128)(2,1)}, u32[]{:S(2)}, u32[]{:S(2)}) collective-permute-start(bf16[1,272,960]{2,1,0:T(8,128)(2,1)} %get-tuple-element.167), channel_id=1, source_target_pairs={{0,3},{1,2},{2,1},{3,0},{4,7},{5,6},{6,5},{7,4},{8,11},{9,10},{10,... | collective-permute-start | bytes 1566728 | tf_op jit(solution)/shard_map/ppermute | solution.py:46
  17.9 30.2 %collective-permute-start.1 = (bf16[1,272,960]{2,1,0:T(8,128)(2,1)}, bf16[1,272,960]{2,1,0:T(8,128)(2,1)}, u32[]{:S(2)}, u32[]{:S(2)}) collective-permute-start(bf16[1,272,960]{2,1,0:T(8,128)(2,1)} %get-tuple-element.168), channel_id=1, source_target_pairs={{0,2},{1,3},{2,0},{3,1},{4,6},{5,7},{6,4},{7,5},{8,10},{9,11},{10,... | collective-permute-start | bytes 1566728 | tf_op jit(solution)/shard_map/ppermute | solution.py:46
  19.0 9.2 %collective-permute-start = (bf16[1,272,960]{2,1,0:T(8,128)(2,1)}, bf16[1,272,960]{2,1,0:T(8,128)(2,1)}, u32[]{:S(2)}, u32[]{:S(2)}) collective-permute-start(bf16[1,272,960]{2,1,0:T(8,128)(2,1)} %get-tuple-element.169), channel_id=1, source_target_pairs={{0,1},{1,0},{2,3},{3,2},{4,5},{5,4},{6,7},{7,6},{8,9},{9,8},{10,11... | collective-permute-start | bytes 1566728 | tf_op jit(solution)/shard_map/ppermute | solution.py:46
  27.8 27.1 %collective-permute-start.4 = (bf16[512,1088]{0,1:T(8,128)(2,1)}, bf16[512,1088]{0,1:T(8,128)(2,1)}, u32[]{:S(2)}, u32[]{:S(2)}) collective-permute-start(bf16[512,1088]{0,1:T(8,128)(2,1)} %pad_maximum_fusion.7), channel_id=1, source_target_pairs={{0,1},{1,0},{2,3},{3,2},{4,5},{5,4},{6,7},{7,6},{8,9},{9,8},{10,11... | collective-permute-start | bytes 3342344 | tf_op jit(solution)/shard_map/ppermute | solution.py:46
  52.1 23.8 %collective-permute-start.9 = (bf16[1,136,1088]{2,1,0:T(8,128)(2,1)S(1)}, bf16[1,136,1088]{2,1,0:T(8,128)(2,1)S(1)}, u32[]{:S(2)}, u32[]{:S(2)}) collective-permute-start(bf16[1,136,1088]{2,1,0:T(8,128)(2,1)S(1)} %get-tuple-element.157), channel_id=1, source_target_pairs={{0,3},{1,2},{2,1},{3,0},{4,7},{5,6},{6,5},{7,4},{8,11},{9,10},{10,... | collective-permute-start | bytes 887816 | tf_op jit(solution)/shard_map/ppermute | solution.py:46
  52.1 23.7 %collective-permute-start.8 = (bf16[1,136,1088]{2,1,0:T(8,128)(2,1)S(1)}, bf16[1,136,1088]{2,1,0:T(8,128)(2,1)S(1)}, u32[]{:S(2)}, u32[]{:S(2)}) collective-permute-start(bf16[1,136,1088]{2,1,0:T(8,128)(2,1)S(1)} %get-tuple-element.158), channel_id=1, source_target_pairs={{0,2},{1,3},{2,0},{3,1},{4,6},{5,7},{6,4},{7,5},{8,10},{9,11},{10,... | collective-permute-start | bytes 887816 | tf_op jit(solution)/shard_map/ppermute | solution.py:46
  53.5 22.4 %collective-permute-start.7 = (bf16[1,272,1088]{2,1,0:T(8,128)(2,1)S(1)}, bf16[1,272,1088]{2,1,0:T(8,128)(2,1)S(1)}, u32[]{:S(2)}, u32[]{:S(2)}) collective-permute-start(bf16[1,272,1088]{2,1,0:T(8,128)(2,1)S(1)} %get-tuple-element.159), channel_id=1, source_target_pairs={{0,1},{1,0},{2,3},{3,2},{4,5},{5,4},{6,7},{7,6},{8,9},{9,8},{10,11... | collective-permute-start | bytes 1775624 | tf_op jit(solution)/shard_map/ppermute | solution.py:46
  81.1 15.7 %collective-permute-start.12 = (bf16[256,1088]{0,1:T(8,128)(2,1)}, bf16[256,1088]{0,1:T(8,128)(2,1)S(1)}, u32[]{:S(2)}, u32[]{:S(2)}) collective-permute-start(bf16[256,1088]{0,1:T(8,128)(2,1)} %bitcast_convert_fusion), channel_id=1, source_target_pairs={{0,2},{1,3},{2,0},{3,1},{4,6},{5,7},{6,4},{7,5},{8,10},{9,11},{10,... | collective-permute-start | bytes 1671176 | tf_op jit(solution)/shard_map/ppermute | solution.py:46
  85.2 22.7 %collective-permute-start.11 = (bf16[256,1088]{0,1:T(8,128)(2,1)S(1)}, bf16[256,1088]{0,1:T(8,128)(2,1)S(1)}, u32[]{:S(2)}, u32[]{:S(2)}) collective-permute-start(bf16[256,1088]{0,1:T(8,128)(2,1)S(1)} %slice.585), channel_id=1, source_target_pairs={{0,2},{1,3},{2,0},{3,1},{4,6},{5,7},{6,4},{7,5},{8,10},{9,11},{10,... | collective-permute-start | bytes 1671176 | tf_op jit(solution)/shard_map/ppermute | solution.py:46
  96.9 27.4 %collective-permute-start.13 = (bf16[512,1088]{0,1:T(8,128)(2,1)S(1)}, bf16[512,1088]{0,1:T(8,128)(2,1)S(1)}, u32[]{:S(2)}, u32[]{:S(2)}) collective-permute-start(bf16[512,1088]{0,1:T(8,128)(2,1)S(1)} %pad_maximum_fusion.8), channel_id=1, source_target_pairs={{0,1},{1,0},{2,3},{3,2},{4,5},{5,4},{6,7},{7,6},{8,9},{9,8},{10,11... | collective-permute-start | bytes 3342344 | tf_op jit(solution)/shard_map/ppermute | solution.py:46
  97.1 26.9 %collective-permute-start.16 = (bf16[2,136,1088]{2,1,0:T(8,128)(2,1)S(1)}, bf16[2,136,1088]{2,1,0:T(8,128)(2,1)S(1)}, u32[]{:S(2)}, u32[]{:S(2)}) collective-permute-start(bf16[2,136,1088]{2,1,0:T(8,128)(2,1)S(1)} %constant_dynamic-update-slice_fusion.11), channel_id=1, source_target_pairs={{0,4},{4,0},{8,12},{12,8},{16,20},{20,16},{24,28},{28,24},{1,5},{5... | collective-permute-start | bytes 1775624 | tf_op jit(solution)/shard_map/ppermute | solution.py:94
  110.1 13.7 %collective-permute-start.14 = (bf16[256,1088]{0,1:T(8,128)(2,1)S(1)}, bf16[256,1088]{0,1:T(8,128)(2,1)S(1)}, u32[]{:S(2)}, u32[]{:S(2)}) collective-permute-start(bf16[256,1088]{0,1:T(8,128)(2,1)S(1)} %add_convert_fusion.6), channel_id=1, source_target_pairs={{0,2},{1,3},{2,0},{3,1},{4,6},{5,7},{6,4},{7,5},{8,10},{9,11},{10,... | collective-permute-start | bytes 1671176 | tf_op jit(solution)/shard_map/ppermute | solution.py:46
  143.6 25.4 %collective-permute-start.17 = (bf16[512,1088]{0,1:T(8,128)(2,1)}, bf16[512,1088]{0,1:T(8,128)(2,1)}, u32[]{:S(2)}, u32[]{:S(2)}) collective-permute-start(bf16[512,1088]{0,1:T(8,128)(2,1)} %slice.580), channel_id=1, source_target_pairs={{0,1},{1,0},{2,3},{3,2},{4,5},{5,4},{6,7},{7,6},{8,9},{9,8},{10,11... | collective-permute-start | bytes 3342344 | tf_op jit(solution)/shard_map/ppermute | solution.py:46
  145.3 68.1 %collective-permute-start.27 = (bf16[48,1088]{1,0:T(8,128)(2,1)}, bf16[48,1088]{1,0:T(8,128)(2,1)}, u32[]{:S(2)}, u32[]{:S(2)}) collective-permute-start(bf16[48,1088]{1,0:T(8,128)(2,1)} %get-tuple-element.199), channel_id=1, source_target_pairs={{1,0},{2,1},{3,2},{5,4},{6,5},{7,6},{9,8},{10,9},{11,10},{13,12},{... | collective-permute-start | bytes 313352 | tf_op jit(solution)/shard_map/ppermute | solution.py:531
  146.6 66.8 %collective-permute-start.26 = (bf16[48,1088]{1,0:T(8,128)(2,1)S(1)}, bf16[48,1088]{1,0:T(8,128)(2,1)}, u32[]{:S(2)}, u32[]{:S(2)}) collective-permute-start(bf16[48,1088]{1,0:T(8,128)(2,1)S(1)} %get-tuple-element.200), channel_id=1, source_target_pairs={{0,1},{1,2},{2,3},{4,5},{5,6},{6,7},{8,9},{9,10},{10,11},{12,13},{... | collective-permute-start | bytes 313352 | tf_op jit(solution)/shard_map/ppermute | solution.py:529
  167.4 30.2 %collective-permute-start.21 = (bf16[1,544,1088]{2,1,0:T(8,128)(2,1)S(1)}, bf16[1,544,1088]{2,1,0:T(8,128)(2,1)S(1)}, u32[]{:S(2)}, u32[]{:S(2)}) collective-permute-start(bf16[1,544,1088]{2,1,0:T(8,128)(2,1)S(1)} %dynamic-slice_bitcast_fusion), channel_id=1, source_target_pairs={{0,4},{4,0},{8,12},{12,8},{16,20},{20,16},{24,28},{28,24},{1,5},{5... | collective-permute-start | bytes 3551240 | tf_op jit(solution)/shard_map/ppermute | solution.py:94
  171.4 15.6 %collective-permute-start.18 = (bf16[256,1088]{0,1:T(8,128)(2,1)S(1)}, bf16[256,1088]{0,1:T(8,128)(2,1)S(1)}, u32[]{:S(2)}, u32[]{:S(2)}) collective-permute-start(bf16[256,1088]{0,1:T(8,128)(2,1)S(1)} %slice.584), channel_id=1, source_target_pairs={{0,2},{1,3},{2,0},{3,1},{4,6},{5,7},{6,4},{7,5},{8,10},{9,11},{10,... | collective-permute-start | bytes 1671176 | tf_op jit(solution)/shard_map/ppermute | solution.py:46
  176.1 29.4 %collective-permute-start.22 = (bf16[4,136,1088]{2,1,0:T(8,128)(2,1)S(1)}, bf16[4,136,1088]{2,1,0:T(8,128)(2,1)S(1)}, u32[]{:S(2)}, u32[]{:S(2)}) collective-permute-start(bf16[4,136,1088]{2,1,0:T(8,128)(2,1)S(1)} %constant_dynamic-slice_fusion.19), channel_id=1, source_target_pairs={{0,8},{4,12},{8,0},{12,4},{16,24},{20,28},{24,16},{28,20},{1,9},{5... | collective-permute-start | bytes 3551240 | tf_op jit(solution)/shard_map/ppermute | solution.py:94
  189.8 15.7 %collective-permute-start.19 = (bf16[256,1088]{0,1:T(8,128)(2,1)S(1)}, bf16[256,1088]{0,1:T(8,128)(2,1)S(1)}, u32[]{:S(2)}, u32[]{:S(2)}) collective-permute-start(bf16[256,1088]{0,1:T(8,128)(2,1)S(1)} %get-tuple-element.151), channel_id=1, source_target_pairs={{0,2},{1,3},{2,0},{3,1},{4,6},{5,7},{6,4},{7,5},{8,10},{9,11},{10,... | collective-permute-start | bytes 1671176 | tf_op jit(solution)/shard_map/ppermute | solution.py:46
  207.2 37.0 %collective-permute-start.23 = (bf16[1,272,1088]{2,1,0:T(8,128)(2,1)}, bf16[1,272,1088]{2,1,0:T(8,128)(2,1)}, u32[]{:S(2)}, u32[]{:S(2)}) collective-permute-start(bf16[1,272,1088]{2,1,0:T(8,128)(2,1)} %constant_dynamic-slice_fusion.18), channel_id=1, source_target_pairs={{0,8},{4,12},{8,0},{12,4},{16,24},{20,28},{24,16},{28,20},{1,9},{5... | collective-permute-start | bytes 1775624 | tf_op jit(solution)/shard_map/ppermute | solution.py:94
  210.2 34.3 %collective-permute-start.24 = (bf16[4,72,1088]{2,1,0:T(8,128)(2,1)}, bf16[4,72,1088]{2,1,0:T(8,128)(2,1)}, u32[]{:S(2)}, u32[]{:S(2)}) collective-permute-start(bf16[4,72,1088]{2,1,0:T(8,128)(2,1)} %constant_dynamic-slice_fusion.17), channel_id=1, source_target_pairs={{0,4},{4,0},{8,12},{12,8},{16,20},{20,16},{24,28},{28,24},{1,5},{5... | collective-permute-start | bytes 1880072 | tf_op jit(solution)/shard_map/ppermute | solution.py:94
  239.0 24.7 %collective-permute-start.32 = (bf16[4,136,544]{2,1,0:T(8,128)(2,1)S(1)}, bf16[4,136,544]{2,1,0:T(8,128)(2,1)S(1)}, u32[]{:S(2)}, u32[]{:S(2)}) collective-permute-start(bf16[4,136,544]{2,1,0:T(8,128)(2,1)S(1)} %constant_dynamic-slice_fusion.11), channel_id=1, source_target_pairs={{0,8},{4,12},{8,0},{12,4},{16,24},{20,28},{24,16},{28,20},{1,9},{5... | collective-permute-start | bytes 1775624 | tf_op jit(solution)/shard_map/ppermute | solution.py:94
  240.4 24.7 %collective-permute-start.31 = (bf16[4,136,544]{2,1,0:T(8,128)(2,1)S(1)}, bf16[4,136,544]{2,1,0:T(8,128)(2,1)S(1)}, u32[]{:S(2)}, u32[]{:S(2)}) collective-permute-start(bf16[4,136,544]{2,1,0:T(8,128)(2,1)S(1)} %constant_dynamic-slice_fusion.12), channel_id=1, source_target_pairs={{0,4},{4,0},{8,12},{12,8},{16,20},{20,16},{24,28},{28,24},{1,5},{5... | collective-permute-start | bytes 1775624 | tf_op jit(solution)/shard_map/ppermute | solution.py:94
  244.2 20.8 %collective-permute-start.33 = (bf16[512,1088]{0,1:T(8,128)(2,1)S(1)}, bf16[512,1088]{0,1:T(8,128)(2,1)S(1)}, u32[]{:S(2)}, u32[]{:S(2)}) collective-permute-start(bf16[512,1088]{0,1:T(8,128)(2,1)S(1)} %slice.578), channel_id=1, source_target_pairs={{0,1},{1,0},{2,3},{3,2},{4,5},{5,4},{6,7},{7,6},{8,9},{9,8},{10,11... | collective-permute-start | bytes 3342344 | tf_op jit(solution)/shard_map/ppermute | solution.py:46
  246.9 18.2 %collective-permute-start.28 = (bf16[1,136,1088]{2,1,0:T(8,128)(2,1)S(1)}, bf16[1,136,1088]{2,1,0:T(8,128)(2,1)S(1)}, u32[]{:S(2)}, u32[]{:S(2)}) collective-permute-start(bf16[1,136,1088]{2,1,0:T(8,128)(2,1)S(1)} %constant_dynamic-slice_fusion.16), channel_id=1, source_target_pairs={{0,16},{4,20},{8,24},{12,28},{16,0},{20,4},{24,8},{28,12},{1,17},{... | collective-permute-start | bytes 887816 | tf_op jit(solution)/shard_map/ppermute | solution.py:94
  249.7 32.1 %collective-permute-start.30 = (bf16[256,1088]{0,1:T(8,128)(2,1)S(1)}, bf16[256,1088]{0,1:T(8,128)(2,1)S(1)}, u32[]{:S(2)}, u32[]{:S(2)}) collective-permute-start(bf16[256,1088]{0,1:T(8,128)(2,1)S(1)} %slice.583), channel_id=1, source_target_pairs={{0,2},{1,3},{2,0},{3,1},{4,6},{5,7},{6,4},{7,5},{8,10},{9,11},{10,... | collective-permute-start | bytes 1671176 | tf_op jit(solution)/shard_map/ppermute | solution.py:46
  263.7 18.0 %collective-permute-start.29 = (bf16[4,40,1088]{2,1,0:T(8,128)(2,1)S(1)}, bf16[4,40,1088]{2,1,0:T(8,128)(2,1)S(1)}, u32[]{:S(2)}, u32[]{:S(2)}) collective-permute-start(bf16[4,40,1088]{2,1,0:T(8,128)(2,1)S(1)} %constant_dynamic-slice_fusion.15), channel_id=1, source_target_pairs={{0,16},{4,20},{8,24},{12,28},{16,0},{20,4},{24,8},{28,12},{1,17},{... | collective-permute-start | bytes 1044488 | tf_op jit(solution)/shard_map/ppermute | solution.py:94
  284.6 7.9 %collective-permute-start.35 = (bf16[1,40,1088]{2,1,0:T(8,128)(2,1)S(1)}, bf16[1,40,1088]{2,1,0:T(8,128)(2,1)S(1)}, u32[]{:S(2)}, u32[]{:S(2)}) collective-permute-start(bf16[1,40,1088]{2,1,0:T(8,128)(2,1)S(1)} %get-tuple-element.209), channel_id=1, source_target_pairs={{0,1},{1,0},{2,3},{3,2},{4,5},{5,4},{6,7},{7,6},{8,9},{9,8},{10,11... | collective-permute-start | bytes 261128 | tf_op jit(solution)/shard_map/ppermute | solution.py:46
  284.8 16.8 %collective-permute-start.34 = (bf16[1,136,1088]{2,1,0:T(8,128)(2,1)S(1)}, bf16[1,136,1088]{2,1,0:T(8,128)(2,1)S(1)}, u32[]{:S(2)}, u32[]{:S(2)}) collective-permute-start(bf16[1,136,1088]{2,1,0:T(8,128)(2,1)S(1)} %add_convert_fusion.10), channel_id=1, source_target_pairs={{0,16},{4,20},{8,24},{12,28},{16,0},{20,4},{24,8},{28,12},{1,17},{... | collective-permute-start | bytes 887816 | tf_op jit(solution)/shard_map/ppermute | solution.py:94
  284.8 16.8 %collective-permute-start.39 = (bf16[4,72,544]{2,1,0:T(8,128)(2,1)S(1)}, bf16[4,72,544]{2,1,0:T(8,128)(2,1)S(1)}, u32[]{:S(2)}, u32[]{:S(2)}) collective-permute-start(bf16[4,72,544]{2,1,0:T(8,128)(2,1)S(1)} %constant_dynamic-slice_fusion.6), channel_id=1, source_target_pairs={{0,4},{4,0},{8,12},{12,8},{16,20},{20,16},{24,28},{28,24},{1,5},{5... | collective-permute-start | bytes 940040 | tf_op jit(solution)/shard_map/ppermute | solution.py:94
  287.7 17.3 %collective-permute-start.38 = (bf16[4,72,544]{2,1,0:T(8,128)(2,1)S(1)}, bf16[4,72,544]{2,1,0:T(8,128)(2,1)S(1)}, u32[]{:S(2)}, u32[]{:S(2)}) collective-permute-start(bf16[4,72,544]{2,1,0:T(8,128)(2,1)S(1)} %constant_dynamic-slice_fusion.7), channel_id=1, source_target_pairs={{0,8},{4,12},{8,0},{12,4},{16,24},{20,28},{24,16},{28,20},{1,9},{5... | collective-permute-start | bytes 940040 | tf_op jit(solution)/shard_map/ppermute | solution.py:94
  289.9 15.2 %collective-permute-start.40 = (bf16[256,1088]{0,1:T(8,128)(2,1)S(1)}, bf16[256,1088]{0,1:T(8,128)(2,1)S(1)}, u32[]{:S(2)}, u32[]{:S(2)}) collective-permute-start(bf16[256,1088]{0,1:T(8,128)(2,1)S(1)} %slice.582), channel_id=1, source_target_pairs={{0,2},{1,3},{2,0},{3,1},{4,6},{5,7},{6,4},{7,5},{8,10},{9,11},{10,... | collective-permute-start | bytes 1671176 | tf_op jit(solution)/shard_map/ppermute | solution.py:46
  307.4 13.7 %collective-permute-start.45 = (f32[4,1088]{1,0:T(4,128)}, f32[4,1088]{1,0:T(4,128)S(1)}, u32[]{:S(2)}, u32[]{:S(2)}) collective-permute-start(f32[4,1088]{1,0:T(4,128)} %pad_maximum_fusion.21), channel_id=1, source_target_pairs={{0,2},{1,3},{2,0},{3,1},{4,6},{5,7},{6,4},{7,5},{8,10},{9,11},{10,... | collective-permute-start | bytes 52232 | tf_op jit(solution)/shard_map/ppermute | solution.py:46
  310.3 23.3 %collective-permute-start.44 = (bf16[4,40,544]{2,1,0:T(8,128)(2,1)}, bf16[4,40,544]{2,1,0:T(8,128)(2,1)}, u32[]{:S(2)}, u32[]{:S(2)}) collective-permute-start(bf16[4,40,544]{2,1,0:T(8,128)(2,1)} %constant_dynamic-slice_fusion.4), channel_id=1, source_target_pairs={{0,16},{4,20},{8,24},{12,28},{16,0},{20,4},{24,8},{28,12},{1,17},{... | collective-permute-start | bytes 522248 | tf_op jit(solution)/shard_map/ppermute | solution.py:94
  310.6 27.4 %collective-permute-start.43 = (bf16[4,40,544]{2,1,0:T(8,128)(2,1)}, bf16[4,40,544]{2,1,0:T(8,128)(2,1)}, u32[]{:S(2)}, u32[]{:S(2)}) collective-permute-start(bf16[4,40,544]{2,1,0:T(8,128)(2,1)} %constant_dynamic-slice_fusion.5), channel_id=1, source_target_pairs={{0,16},{4,20},{8,24},{12,28},{16,0},{20,4},{24,8},{28,12},{1,17},{... | collective-permute-start | bytes 522248 | tf_op jit(solution)/shard_map/ppermute | solution.py:94
  314.3 30.9 %collective-permute-start.42 = (bf16[1,40,4352]{2,1,0:T(8,128)(2,1)S(1)}, bf16[1,40,4352]{2,1,0:T(8,128)(2,1)S(1)}, u32[]{:S(2)}, u32[]{:S(2)}) collective-permute-start(bf16[1,40,4352]{2,1,0:T(8,128)(2,1)S(1)} %bitcast.144), channel_id=1, source_target_pairs={{0,16},{4,20},{8,24},{12,28},{16,0},{20,4},{24,8},{28,12},{1,17},{... | collective-permute-start | bytes 1044488 | tf_op jit(solution)/shard_map/ppermute | solution.py:94
  315.9 31.2 %collective-permute-start.41 = (bf16[1,272,1088]{2,1,0:T(8,128)(2,1)S(1)}, bf16[1,272,1088]{2,1,0:T(8,128)(2,1)S(1)}, u32[]{:S(2)}, u32[]{:S(2)}) collective-permute-start(bf16[1,272,1088]{2,1,0:T(8,128)(2,1)S(1)} %pad_maximum_fusion.15), channel_id=1, source_target_pairs={{0,8},{4,12},{8,0},{12,4},{16,24},{20,28},{24,16},{28,20},{1,9},{5... | collective-permute-start | bytes 1775624 | tf_op jit(solution)/shard_map/ppermute | solution.py:94
  349.6 41.0 %collective-permute-start.46 = (bf16[1,544,1088]{2,1,0:T(8,128)(2,1)S(1)}, bf16[1,544,1088]{2,1,0:T(8,128)(2,1)}, u32[]{:S(2)}, u32[]{:S(2)}) collective-permute-start(bf16[1,544,1088]{2,1,0:T(8,128)(2,1)S(1)} %pad_maximum_fusion.5), channel_id=1, source_target_pairs={{0,4},{4,0},{8,12},{12,8},{16,20},{20,16},{24,28},{28,24},{1,5},{5... | collective-permute-start | bytes 3551240 | tf_op jit(solution)/shard_map/ppermute | solution.py:94
  351.1 39.5 %collective-permute-start.47 = (bf16[1,72,4352]{2,1,0:T(8,128)(2,1)S(1)}, bf16[1,72,4352]{2,1,0:T(8,128)(2,1)S(1)}, u32[]{:S(2)}, u32[]{:S(2)}) collective-permute-start(bf16[1,72,4352]{2,1,0:T(8,128)(2,1)S(1)} %pad_maximum_fusion.13), channel_id=1, source_target_pairs={{0,4},{4,0},{8,12},{12,8},{16,20},{20,16},{24,28},{28,24},{1,5},{5... | collective-permute-start | bytes 1880072 | tf_op jit(solution)/shard_map/ppermute | solution.py:94
  391.7 10.0 %collective-permute-start.55 = (f32[3264]{0:T(1024)S(1)}, f32[3264]{0:T(1024)S(1)}, u32[]{:S(2)}, u32[]{:S(2)}) collective-permute-start(f32[3264]{0:T(1024)S(1)} %concatenate.143), channel_id=1, source_target_pairs={{0,4},{4,0},{8,12},{12,8},{16,20},{20,16},{24,28},{28,24},{1,5},{5... | collective-permute-start | bytes 39176 | tf_op jit(solution)/shard_map/ppermute | solution.py:94
  393.6 12.3 %collective-permute-start.53 = (bf16[1,40,2176]{2,1,0:T(8,128)(2,1)S(1)}, bf16[1,40,2176]{2,1,0:T(8,128)(2,1)S(1)}, u32[]{:S(2)}, u32[]{:S(2)}) collective-permute-start(bf16[1,40,2176]{2,1,0:T(8,128)(2,1)S(1)} %bitcast.154), channel_id=1, source_target_pairs={{0,16},{4,20},{8,24},{12,28},{16,0},{20,4},{24,8},{28,12},{1,17},{... | collective-permute-start | bytes 522248 | tf_op jit(solution)/shard_map/ppermute | solution.py:94
  394.1 14.4 %collective-permute-start.54 = (bf16[1,40,2176]{2,1,0:T(8,128)(2,1)S(1)}, bf16[1,40,2176]{2,1,0:T(8,128)(2,1)S(1)}, u32[]{:S(2)}, u32[]{:S(2)}) collective-permute-start(bf16[1,40,2176]{2,1,0:T(8,128)(2,1)S(1)} %bitcast.156), channel_id=1, source_target_pairs={{0,16},{4,20},{8,24},{12,28},{16,0},{20,4},{24,8},{28,12},{1,17},{... | collective-permute-start | bytes 522248 | tf_op jit(solution)/shard_map/ppermute | solution.py:94
  397.2 31.7 %collective-permute-start.52 = (bf16[1,136,4352]{2,1,0:T(8,128)(2,1)S(1)}, bf16[1,136,4352]{2,1,0:T(8,128)(2,1)S(1)}, u32[]{:S(2)}, u32[]{:S(2)}) collective-permute-start(bf16[1,136,4352]{2,1,0:T(8,128)(2,1)S(1)} %pad_maximum_fusion.6), channel_id=1, source_target_pairs={{0,8},{4,12},{8,0},{12,4},{16,24},{20,28},{24,16},{28,20},{1,9},{5... | collective-permute-start | bytes 3551240 | tf_op jit(solution)/shard_map/ppermute | solution.py:94
  431.2 9.6 %collective-permute-start.57 = (bf16[1,72,2176]{2,1,0:T(8,128)(2,1)S(1)}, bf16[1,72,2176]{2,1,0:T(8,128)(2,1)S(1)}, u32[]{:S(2)}, u32[]{:S(2)}) collective-permute-start(bf16[1,72,2176]{2,1,0:T(8,128)(2,1)S(1)} %pad_maximum_fusion.19), channel_id=1, source_target_pairs={{0,4},{4,0},{8,12},{12,8},{16,20},{20,16},{24,28},{28,24},{1,5},{5... | collective-permute-start | bytes 940040 | tf_op jit(solution)/shard_map/ppermute | solution.py:94
  441.2 10.0 %collective-permute-start.59 = (bf16[1,136,2176]{2,1,0:T(8,128)(2,1)S(1)}, bf16[1,136,2176]{2,1,0:T(8,128)(2,1)S(1)}, u32[]{:S(2)}, u32[]{:S(2)}) collective-permute-start(bf16[1,136,2176]{2,1,0:T(8,128)(2,1)S(1)} %pad_maximum_fusion.16), channel_id=1, source_target_pairs={{0,4},{4,0},{8,12},{12,8},{16,20},{20,16},{24,28},{28,24},{1,5},{5... | collective-permute-start | bytes 1775624 | tf_op jit(solution)/shard_map/ppermute | solution.py:94
  441.5 10.6 %collective-permute-start.60 = (bf16[1,136,2176]{2,1,0:T(8,128)(2,1)S(1)}, bf16[1,136,2176]{2,1,0:T(8,128)(2,1)S(1)}, u32[]{:S(2)}, u32[]{:S(2)}) collective-permute-start(bf16[1,136,2176]{2,1,0:T(8,128)(2,1)S(1)} %pad_maximum_fusion.17), channel_id=1, source_target_pairs={{0,8},{4,12},{8,0},{12,4},{16,24},{20,28},{24,16},{28,20},{1,9},{5... | collective-permute-start | bytes 1775624 | tf_op jit(solution)/shard_map/ppermute | solution.py:94
  (88 other events, 838.5 us)
where the time goes:
time: 467 us; the launch traced here: 459 us
  waiting for transfers between devices  219 us (47%)
  starting transfers between devices  68.9 us (15%)
  other arithmetic  52.9 us (11%)
  local copies, waits for them, and re-layouts  52.8 us (11%)
  matrix products  41.1 us (9%)
  Pallas kernels  21.1 us (5%)
    ppermute x28, waiting for transfers between devices, swap_rep(): return lax.ppermute(values, 'rep', [(i, i ^ bit) for i in range(size)])  151 us
    ppermute x32, waiting for transfers between devices, swap(): return lax.ppermute(values, 'shard', [(i, i ^ bit) for i in range(size)])  68.1 us
    dot_general x13, matrix products, contract(): lax.dot_general(left, right, (((left_dim,), (right_dim,)), ((), ())), pre...  41.1 us
    ppermute x28, starting transfers between devices, swap_rep(): return lax.ppermute(values, 'rep', [(i, i ^ bit) for i in range(size)])  32.5 us
    ppermute x32, starting transfers between devices, swap(): return lax.ppermute(values, 'shard', [(i, i ^ bit) for i in range(size)])  21.2 us
    ppermute x1, starting transfers between devices, local(): lax.ppermute(attention_output_weight[own - pad:], 'shard', to_right)  13.9 us
    unnamed x151, local copies, waits for them, and re-layouts  10.7 us
    pallas_call x1, Pallas kernels, attend_backward(): pl.pallas_call(functools.partial(backward_kernel, blocks, block), grid_sp...  10.6 us
  transfers between devices with their start and end apart: 62, of which 30 were waited for; matrix products, arithmetic and copies ran while one was open for 22% of the time, Pallas kernels for 5%

commit v1 on v0

--- a/solution.py
+++ b/solution.py
@@ -103,21 +103,25 @@
 
 
 def after(values, gate):
-    return lax.optimization_barrier((values, gate))[0]
+    return lax.optimization_barrier((values, gate))
 
 
 def half_window(rows):
     return min(rows, (rows + 15) // 16 * 8)
 
 
-def halve(values, bit):
+def half_of(values, index):
     rows = values.shape[1]
     window = half_window(rows)
-    mine = (lax.axis_index("rep") // bit) % 2
-    far = rows - window
-    send = lax.dynamic_slice_in_dim(values, (1 - mine) * far, window, 1)
-    keep = lax.dynamic_slice_in_dim(values, mine * far, window, 1)
-    return keep, swap_rep(send, bit)
+    return lax.dynamic_slice_in_dim(values, index * (rows - window), window, 1)
+
+
+def sent_half(values, bit):
+    return swap_rep(half_of(values, 1 - (lax.axis_index("rep") // bit) % 2), bit)
+
+
+def kept_half(values, bit):
+    return half_of(values, (lax.axis_index("rep") // bit) % 2)
 
 
 def add(keep, other):
@@ -135,37 +139,44 @@
 class Chain:
     def __init__(self, steps):
         self.steps = steps
-        self.result = None
         self.take(None)
 
     def take(self, got):
         try:
-            self.waits = self.steps.send(got)
+            self.waits, self.holds = self.steps.send(got)
         except StopIteration as end:
-            self.waits = None
-            self.result = end.value
-
-
-def advance(chains, gate=()):
-    live = [c for c in chains if c.waits is not None]
-    arrived, _ = lax.optimization_barrier((tuple(c.waits for c in live), gate))
-    for chain, got in zip(live, arrived):
-        chain.take(got)
+            self.waits, self.holds = None, end.value
+
+    def advance(self, previous, gate=()):
+        if self.waits is not None:
+            if previous is self:
+                waits, gate = after(self.waits, gate)
+            else:
+                waits, (previous.holds, gate) = after(self.waits, (previous.holds, gate))
+            self.take((waits, self.holds))
+        return gate
 
 
 def scatter_steps(lanes, orders):
     sizes = []
     for step in range(len(orders[0])):
         sizes.append(lanes[0].shape[1])
-        halves = [halve(v, order[step]) for v, order in zip(lanes, orders)]
-        others = yield tuple(h[1] for h in halves)
-        lanes = [add(h[0], other) for h, other in zip(halves, others)]
+        others, held = yield (
+            tuple(sent_half(v, order[step]) for v, order in zip(lanes, orders)),
+            tuple(lanes),
+        )
+        lanes = [
+            add(kept_half(v, order[step]), other) for v, other, order in zip(held, others, orders)
+        ]
     return list(lax.optimization_barrier(tuple(lanes))), sizes
 
 
 def gather_steps(lanes, orders, sizes):
     for step in reversed(range(len(orders[0]))):
-        others = yield tuple(swap_rep(v, order[step]) for v, order in zip(lanes, orders))
+        others, lanes = yield (
+            tuple(swap_rep(v, order[step]) for v, order in zip(lanes, orders)),
+            tuple(lanes),
+        )
         lanes = [
             join(v, other, order[step], sizes[step])
             for v, other, order in zip(lanes, others, orders)
@@ -177,9 +188,9 @@
     size = lax.axis_size("shard")
     index = lax.axis_index("shard")
     pieces = [lax.dynamic_index_in_dim(blocks, index ^ o, 0, keepdims=True) for o in range(size)]
-    others = yield tuple(swap(pieces[o], o) for o in range(1, size))
+    others, first = yield tuple(swap(pieces[o], o) for o in range(1, size)), pieces[0]
     result = jnp.zeros_like(blocks)
-    for o, piece in enumerate(pieces[:1] + list(others)):
+    for o, piece in enumerate((first,) + tuple(others)):
         result = lax.dynamic_update_slice_in_dim(result, piece, index ^ o, 0)
     return [result[i] for i in range(size)]
 
@@ -217,18 +228,18 @@
 def shard_sum(parts):
     for bit in reversed(bits_far_first()):
         half = parts.shape[0] // 2
-        (other,) = yield (swap(parts[half:].astype(low), bit),)
-        parts = parts[:half] + other.astype(f32)
+        (other,), kept = yield (swap(parts[half:].astype(low), bit),), parts[:half]
+        parts = kept + other.astype(f32)
     return parts
 
 
 def vector_sum(partial, complete, own_part):
     for bit in bits_far_first():
-        (other,) = yield (swap(partial, bit),)
+        (other,), partial = yield (swap(partial, bit),), partial
         partial = partial + other
     total = jnp.concatenate([own_part(p) for p in partial] + complete)
     for bit in rep_bits(False):
-        (other,) = yield (swap_rep(total, bit),)
+        (other,), total = yield (swap_rep(total, bit),), total
         total = total + other
     return total
 
@@ -520,23 +531,16 @@
         )
     ).reshape(width, 3 * window)
     up_blocks = jnp.stack([up_weight[:, s * hidden : (s + 1) * hidden] for s in range(shards)])
-    up_pieces = send_halves(after(up_blocks, weight_in))
+    up_blocks, weight_in = after(up_blocks, weight_in)
+    up_pieces = send_halves(up_blocks)
     to_right = [(i, i + 1) for i in range(shards - 1)]
     to_left = [(i + 1, i) for i in range(shards - 1)]
-    weight_out_window = lax.dynamic_slice_in_dim(
-        jnp.concatenate(
-            [
-                lax.ppermute(attention_output_weight[own - pad :], "shard", to_right),
-                attention_output_weight,
-                lax.ppermute(attention_output_weight[:pad], "shard", to_left),
-            ],
-            axis=0,
-        ),
-        pad - skew,
-        window,
-        0,
-    )
-    branch = gather_relative(after(cotangent.reshape(seqs * span, width).astype(low), up_pieces))
+    edges = (
+        lax.ppermute(attention_output_weight[own - pad :], "shard", to_right),
+        lax.ppermute(attention_output_weight[:pad], "shard", to_left),
+    )
+    own_branch, up_pieces = after(cotangent.reshape(seqs * span, width).astype(low), up_pieces)
+    branch = gather_relative(own_branch)
     grad_out = cotangent.reshape(seqs * span, width)
 
     def own_rows(values):
@@ -569,7 +573,13 @@
     projected_parts = per_sequence(projected) if seqs > 1 else [projected]
     forward_parts = [attend_forward(place, p, heads, span) for p in projected_parts]
     attended = join_sequences([p[1] for p in forward_parts])
-    attended, up_pieces = lax.optimization_barrier((attended, up_pieces))
+    attended, up_pieces, edges = lax.optimization_barrier((attended, up_pieces, edges))
+    weight_out_window = lax.dynamic_slice_in_dim(
+        jnp.concatenate([edges[0], attention_output_weight, edges[1]], axis=0),
+        pad - skew,
+        window,
+        0,
+    )
     attended = own_rows(attended)
     weight_up = join_halves(up_pieces).reshape(width, hidden)
     mixed_sum = scatter_relative(
@@ -583,24 +593,31 @@
     before = contract(hidden_two, weight_up, 1, 0) + up_bias
     activated, slope = gelu_parts(before)
     activated = activated.astype(low)
-    grad_before = (contract(branch, down_weight, 1, 1) * slope).astype(low)
+    down_weight_grad = contract(activated, branch, 0, 0).astype(low)[None]
+    near, far = rep_bits(False), rep_bits(True)
+    down_chain = Chain(plain_sum(down_weight_grad, near))
+    late_branch, down_chain.holds = after(branch, down_chain.holds)
+    grad_before = (contract(late_branch, down_weight, 1, 1) * slope).astype(low)
     hidden_two_sum = contract(grad_before, weight_up, 1, 1)
     hidden_two_sum, late_before, late_active = lax.optimization_barrier(
         (hidden_two_sum, grad_before, activated)
     )
     grad_hidden_two = scatter_relative(hidden_two_sum)
-    down_weight_grad = contract(late_active, branch, 0, 0).astype(low)[None]
     up_weight_grad = contract(hidden_two, late_before, 0, 0).astype(low)
     up_weight_grad = up_weight_grad.reshape(shards, own, hidden)
     down_sum = contract(late_active, down_weight, 1, 0)
     grad_middle = grad_out + norm_back(grad_hidden_two, normed_two, inverse_two, gain_two)
-    near, far = rep_bits(False), rep_bits(True)
-    down_chain = Chain(plain_sum(down_weight_grad, near))
-    up_chain = Chain(turned_sum(up_weight_grad, far))
-    advance([down_chain, up_chain], grad_middle)
+    up_chain = Chain(turned_sum(up_weight_grad, near))
+    down_chain.advance(up_chain)
+    late_middle = down_chain.advance(down_chain, grad_middle)
 
     grad_mixed = gather_relative(grad_middle.astype(low))
+    late_mixed = up_chain.advance(down_chain, grad_mixed)
+    down_chain.advance(up_chain)
     grad_attended = contract(weight_out_window, grad_mixed, 1, 1).astype(low)
+    grad_attended, (down_chain.holds, up_chain.holds) = after(
+        grad_attended, (down_chain.holds, up_chain.holds)
+    )
     grad_parts = per_sequence(grad_attended) if seqs > 1 else [grad_attended]
     backward_parts = [
         attend_backward(place, p, g, f[0], f[2], heads, span)
@@ -617,8 +634,10 @@
         [jnp.where(mine, g, jnp.zeros_like(g)) for g in (grad_query, grad_key, grad_value)], axis=0
     )
     output_weight_grad = contract(attended, grad_mixed, 1, 0).astype(low)
-    block_chain = Chain(shard_sum(after(down_sum, grad_mixed)))
-    advance([down_chain, up_chain, block_chain], grad_query)
+    down_sum, late_mixed = after(down_sum, late_mixed)
+    block_chain = Chain(shard_sum(down_sum))
+    late_query = up_chain.advance(down_chain, own_query)
+    down_chain.advance(up_chain)
 
     def by_owner(gradient):
         return gradient.reshape(shards, own, gradient.shape[1])
@@ -631,13 +650,17 @@
     second_part = jnp.concatenate([second_part, output_blocks], axis=2)
     mixer_chain = Chain(mixer_sum(first_part, second_part, [near, far], own))
     hidden_chain = Chain(shard_sum(contract(grad_projected, weight_in, 0, 1)))
-    chains = [down_chain, up_chain, block_chain, mixer_chain, hidden_chain]
-    while hidden_chain.waits is not None:
-        advance(chains)
-    block_output = middle + block_chain.result + bias_down
-    grad_hidden_one = hidden_chain.result
+    chain = down_chain
+    for step in (
+        [block_chain, hidden_chain, up_chain, down_chain, up_chain, mixer_chain, hidden_chain]
+        + [block_chain, hidden_chain] * shards
+    ):
+        step.advance(chain)
+        chain = step
+    block_output = middle + block_chain.holds + bias_down
+    grad_hidden_one = hidden_chain.holds
     normed_one, inverse_one = normalize(layer_input)
-    input_grad = grad_middle + norm_back(grad_hidden_one, normed_one, inverse_one, gain_one)
+    input_grad = late_middle + norm_back(grad_hidden_one, normed_one, inverse_one, gain_one)
 
     def own_part(values):
         return lax.dynamic_slice_in_dim(values, index * own, own, 0)
@@ -654,22 +677,29 @@
         vector_sum(
             partial,
             [
-                jnp.sum(own_query.astype(f32), axis=1),
+                jnp.sum(late_query.astype(f32), axis=1),
                 jnp.sum(own_value.astype(f32), axis=1),
-                own_part(jnp.sum(grad_mixed.astype(f32), axis=0)),
+                own_part(jnp.sum(late_mixed.astype(f32), axis=0)),
                 own_part(jnp.sum(branch.astype(f32), axis=0)),
                 jnp.sum(grad_before.astype(f32), axis=0),
             ],
             own_part,
         )
     )
-    chains.append(vector_chain)
-    while any(c.waits is not None for c in chains):
-        advance(chains)
-    complete = vector_chain.result
-    down_weight_grad = down_chain.result[0]
-    up_weight_grad = up_chain.result
-    first_part, second_part = mixer_chain.result
+    down, up, mixer, vector = chains = [down_chain, up_chain, mixer_chain, vector_chain]
+    chain = up
+    for step in (
+        [vector, vector, up, mixer, vector, vector, vector, mixer]
+        + [down, up, mixer, mixer, up, mixer]
+        + chains * 8
+    ):
+        if step.waits is not None:
+            step.advance(chain)
+            chain = step
+    complete = vector_chain.holds
+    down_weight_grad = down_chain.holds[0]
+    up_weight_grad = up_chain.holds
+    first_part, second_part = mixer_chain.holds
     input_weight_grad = jnp.concatenate([first_part, second_part[:, :width]], axis=1)
     output_weight_grad = second_part[:, width:]
     (

time: 467 us -> 473 us (1.013)
  starting transfers between devices: 68.9 us -> 59.8 us
  other arithmetic: 52.9 us -> 61.1 us
  waiting for transfers between devices: 219 us -> 211 us
  matrix products: 41.1 us -> 48.9 us
  local copies, waits for them, and re-layouts: 52.8 us -> 59.6 us
    ppermute x28, waiting for transfers between devices: 151 us -> 118 us  [swap_rep(): return lax.ppermute(values, 'rep', [(i, i ^ bit) for i in range(size)])]
    ppermute x32, waiting for transfers between devices: 68.1 us -> 93 us  [swap(): return lax.ppermute(values, 'shard', [(i, i ^ bit) for i in range(size)])]
    ppermute x1, starting transfers between devices: 13.9 us -> 2.99 us  [local(): lax.ppermute(attention_output_weight[own - pad:], 'shard', to_right)]
    dot_general x13, matrix products: 41.1 us -> 48.9 us  [contract(): lax.dot_general(left, right, (((left_dim,), (right_dim,)), ((), ())), pre...]
    unnamed x151 -> x145, local copies, waits for them, and re-layouts: 10.7 us -> 15.6 us
  transfers between devices with their start and end apart: 62 -> 62, of which waited for: 30 -> 27; matrix products, arithmetic and copies ran while one was open for 22% -> 25% of each run, Pallas kernels for 5% -> 5%
where the time goes in v1:
time: 473 us; the launch traced here: 464 us
  waiting for transfers between devices  211 us (45%)
  other arithmetic  61.1 us (13%)
  starting transfers between devices  59.8 us (13%)
  local copies, waits for them, and re-layouts  59.6 us (13%)
  matrix products  48.9 us (10%)
  Pallas kernels  21.1 us (4%)
    ppermute x28, waiting for transfers between devices, swap_rep(): return lax.ppermute(values, 'rep', [(i, i ^ bit) for i in range(size)])  118 us
    ppermute x32, waiting for transfers between devices, swap(): return lax.ppermute(values, 'shard', [(i, i ^ bit) for i in range(size)])  93 us
    dot_general x13, matrix products, contract(): lax.dot_general(left, right, (((left_dim,), (right_dim,)), ((), ())), pre...  48.9 us
    ppermute x28, starting transfers between devices, swap_rep(): return lax.ppermute(values, 'rep', [(i, i ^ bit) for i in range(size)])  36.4 us
    ppermute x32, starting transfers between devices, swap(): return lax.ppermute(values, 'shard', [(i, i ^ bit) for i in range(size)])  19.1 us
    unnamed x145, local copies, waits for them, and re-layouts  15.6 us
    pallas_call x1, Pallas kernels, attend_backward(): pl.pallas_call(functools.partial(backward_kernel, blocks, block), grid_sp...  10.6 us
    pallas_call x1, Pallas kernels, attend_forward(): pl.pallas_call(functools.partial(forward_kernel, blocks, block), grid_spe...  10.5 us
  transfers between devices with their start and end apart: 62, of which 27 were waited for; matrix products, arithmetic and copies ran while one was open for 25% of the time, Pallas kernels for 5%

profile of v1, /device:TPU:0, one launch (start us, length us, event | category | flops | bytes accessed | tf_op | source)
XLA Modules:
  0.0 464.2 jit_solution(10474088706461077305)
XLA Ops:
  6.9 2.9 collective-permute-start.5
  14.6 3.2 fusion.73
  31.5 2.3 pad_maximum_fusion.8
  33.7 19.6 %collective-permute-done.1 = bf16[1,272,960]{2,1,0:T(8,128)(2,1)S(1)} collective-permute-done((bf16[1,272,960]{2,1,0:T(8,128)(2,1)}, bf16[1,272,960]{2,1,0:T(8,128)(2,1)S(1)}, u32[]{:S(2)}, u32[]{:S(2)}) %collective-permute-start.1) | collective-permute-done | bytes 522272 | tf_op jit(solution)/shard_map/ppermute | solution.py:46
  61.0 6.4 %collective-permute-done.9 = bf16[1,136,1088]{2,1,0:T(8,128)(2,1)S(1)} collective-permute-done((bf16[1,136,1088]{2,1,0:T(8,128)(2,1)}, bf16[1,136,1088]{2,1,0:T(8,128)(2,1)S(1)}, u32[]{:S(2)}, u32[]{:S(2)}) %collective-permute-start.9) | collective-permute-done | bytes 295968 | tf_op jit(solution)/shard_map/ppermute | solution.py:46
  67.4 3.0 collective-permute-start.10
  70.4 4.5 collective-permute-done.8
  78.7 2.3 fusion.5
  82.4 2.8 add_convert_fusion.q_ref.k_ref.v_ref
  85.3 10.5 %attend_forward.1 = (f32[320,1024]{1,0:T(8,128)S(1)}, bf16[320,1024]{1,0:T(8,128)(2,1)S(1)}, f32[5,1,1024]{2,1,0:T(1,128)S(1)}) custom-call(s32[4]{0:T(128)S(1)} %gather_fusion, bf16[960,1024]{1,0:T(8,128)(2,1)S(1)} %add_convert_fusion.q_ref.k_ref.v_ref, bf16[960,1024]{1,0:T(8,128)(2,1)S(1)} %add_convert_fusion.q_ref.k_ref.v_ref, ...), custom_call_target="tpu_custom_call" | custom-call | flops 1342177280 | bytes 3932160 | tf_op jit(solution)/shard_map/attend_forward/pallas_call | solution.py:394
  103.0 2.3 slice_add_fusion.1
  106.9 9.9 %collective-permute-done.14 = bf16[256,1088]{0,1:T(8,128)(2,1)S(1)} collective-permute-done((bf16[256,1088]{0,1:T(8,128)(2,1)}, bf16[256,1088]{0,1:T(8,128)(2,1)S(1)}, u32[]{:S(2)}, u32[]{:S(2)}) %collective-permute-start.14) | collective-permute-done | bytes 557088 | tf_op jit(solution)/shard_map/ppermute | solution.py:46
  119.6 8.8 %collective-permute-done.13 = bf16[256,1088]{0,1:T(8,128)(2,1)S(1)} collective-permute-done((bf16[256,1088]{0,1:T(8,128)(2,1)S(1)}, bf16[256,1088]{0,1:T(8,128)(2,1)S(1)}, u32[]{:S(2)}, u32[]{:S(2)}) %collective-permute-start.13) | collective-permute-done | bytes 557088 | tf_op jit(solution)/shard_map/ppermute | solution.py:46
  132.3 12.1 %collective-permute-done.16 = bf16[256,1088]{0,1:T(8,128)(2,1)S(1)} collective-permute-done((bf16[256,1088]{0,1:T(8,128)(2,1)S(1)}, bf16[256,1088]{0,1:T(8,128)(2,1)S(1)}, u32[]{:S(2)}, u32[]{:S(2)}) %collective-permute-start.16) | collective-permute-done | bytes 557088 | tf_op jit(solution)/shard_map/ppermute | solution.py:46
  147.3 3.8 multiply_convert_fusion
  151.2 4.4 convolution_convert_fusion.1
  155.5 15.5 %convert_reduce_fusion.1 = (f32[1088]{0:T(1024)}, bf16[1024,1088]{0,1:T(8,128)(2,1)S(1)}) fusion(f32[1024,1088]{0,1:T(8,128)S(1)} %get-tuple-element.328, bf16[1088,1088]{1,0:T(8,128)(2,1)S(1)} %copy-done, bf16[1024,1088]{0,1:T(8,128)(2,1)S(1)} %constant_dynamic-update-slice_fusion.15), kind=kOutput, calls=%fused_computation.18 | convolution fusion | flops 2437676032 | bytes 11284736 | tf_op jit(solution)/shard_map/dot_general | solution.py:39
  171.0 3.1 fusion.82
  187.5 3.3 convolution_convert_fusion
  191.2 22.3 %collective-permute-done.24 = bf16[1,544,1088]{2,1,0:T(8,128)(2,1)S(1)} collective-permute-done((bf16[1,544,1088]{2,1,0:T(8,128)(2,1)S(1)}, bf16[1,544,1088]{2,1,0:T(8,128)(2,1)S(1)}, u32[]{:S(2)}, u32[]{:S(2)}) %collective-permute-start.24) | collective-permute-done | bytes 1183776 | tf_op jit(solution)/shard_map/ppermute | solution.py:94
  218.7 10.5 %collective-permute-done.21 = bf16[256,1088]{0,1:T(8,128)(2,1)S(1)} collective-permute-done((bf16[256,1088]{0,1:T(8,128)(2,1)S(1)}, bf16[256,1088]{0,1:T(8,128)(2,1)S(1)}, u32[]{:S(2)}, u32[]{:S(2)}) %collective-permute-start.21) | collective-permute-done | bytes 557088 | tf_op jit(solution)/shard_map/ppermute | solution.py:46
  229.4 4.7 %fusion.81 = f32[1024,1088]{0,1:T(8,128)} fusion(bf16[1024,1088]{0,1:T(8,128)(2,1)S(1)} %copy-done.68, bf16[1088,1088]{1,0:T(8,128)(2,1)S(1)} %copy-done), kind=kOutput, calls=%fused_computation.309 | convolution fusion | flops 2424307712 | bytes 9052160 | tf_op jit(solution)/shard_map/dot_general | solution.py:39
  234.4 2.7 collective-permute-start.26
  243.0 8.8 %collective-permute-done.26 = bf16[1,136,1088]{2,1,0:T(8,128)(2,1)S(1)} collective-permute-done((bf16[1,136,1088]{2,1,0:T(8,128)(2,1)S(1)}, bf16[1,136,1088]{2,1,0:T(8,128)(2,1)S(1)}, u32[]{:S(2)}, u32[]{:S(2)}) %collective-permute-start.26) | collective-permute-done | bytes 295968 | tf_op jit(solution)/shard_map/ppermute | solution.py:94
  254.8 10.6 %attend_backward.1 = (bf16[320,1024]{1,0:T(8,128)(2,1)S(1)}, bf16[320,1024]{1,0:T(8,128)(2,1)S(1)}, bf16[320,1024]{1,0:T(8,128)(2,1)S(1)}) custom-call(s32[4]{0:T(128)S(1)} %gather_fusion, bf16[960,1024]{1,0:T(8,128)(2,1)S(1)} %copy-done.3, bf16[960,1024]{1,0:T(8,128)(2,1)S(1)} %copy-done.3, bf16[960,1024]{1,0:T(8,128)(2,1)S(1)} %copy-done.3, ...), custom_call_target="tpu_custom_call" | custom-call | flops 3355443200 | bytes 6553600 | tf_op jit(solution)/shard_map/attend_backward/pallas_call | solution.py:431
  270.5 2.7 convolution_convert_fusion.2
  273.2 2.6 copy.35
  279.0 3.9 collective-permute-start.30
  288.1 2.5 fusion.11
  293.6 5.1 %collective-permute-done.30 = bf16[4,72,1088]{2,1,0:T(8,128)(2,1)S(1)} collective-permute-done((bf16[4,72,1088]{2,1,0:T(8,128)(2,1)S(1)}, bf16[4,72,1088]{2,1,0:T(8,128)(2,1)S(1)}, u32[]{:S(2)}, u32[]{:S(2)}) %collective-permute-start.30) | collective-permute-done | bytes 626720 | tf_op jit(solution)/shard_map/ppermute | solution.py:94
  307.1 13.9 %collective-permute-done.32 = bf16[4,40,1088]{2,1,0:T(8,128)(2,1)S(1)} collective-permute-done((bf16[4,40,1088]{2,1,0:T(8,128)(2,1)S(1)}, bf16[4,40,1088]{2,1,0:T(8,128)(2,1)S(1)}, u32[]{:S(2)}, u32[]{:S(2)}) %collective-permute-start.32) | collective-permute-done | bytes 348192 | tf_op jit(solution)/shard_map/ppermute | solution.py:94
  322.4 11.8 %collective-permute-done.36 = bf16[1,272,1088]{2,1,0:T(8,128)(2,1)S(1)} collective-permute-done((bf16[1,272,1088]{2,1,0:T(8,128)(2,1)S(1)}, bf16[1,272,1088]{2,1,0:T(8,128)(2,1)S(1)}, u32[]{:S(2)}, u32[]{:S(2)}) %collective-permute-start.36) | collective-permute-done | bytes 591904 | tf_op jit(solution)/shard_map/ppermute | solution.py:94
  344.8 6.4 %collective-permute-done.33 = bf16[256,1088]{0,1:T(8,128)(2,1)} collective-permute-done((bf16[256,1088]{0,1:T(8,128)(2,1)}, bf16[256,1088]{0,1:T(8,128)(2,1)}, u32[]{:S(2)}, u32[]{:S(2)}) %collective-permute-start.33) | collective-permute-done | bytes 557088 | tf_op jit(solution)/shard_map/ppermute | solution.py:46
  354.1 8.7 %collective-permute-done.31 = bf16[256,1088]{0,1:T(8,128)(2,1)} collective-permute-done((bf16[256,1088]{0,1:T(8,128)(2,1)}, bf16[256,1088]{0,1:T(8,128)(2,1)}, u32[]{:S(2)}, u32[]{:S(2)}) %collective-permute-start.31) | collective-permute-done | bytes 557088 | tf_op jit(solution)/shard_map/ppermute | solution.py:46
  363.9 3.5 collective-permute-done.43
  371.2 4.1 collective-permute-done.41
  380.0 2.5 collective-permute-start.45
  383.0 2.3 add_bitcast_fusion
  386.1 13.7 %collective-permute-done.49 = f32[3264]{0:T(1024)S(1)} collective-permute-done((f32[3264]{0:T(1024)S(1)}, f32[3264]{0:T(1024)S(1)}, u32[]{:S(2)}, u32[]{:S(2)}) %collective-permute-start.49) | collective-permute-done | bytes 13088 | tf_op jit(solution)/shard_map/ppermute | solution.py:94
  405.1 3.0 collective-permute-done.54
  410.6 3.0 collective-permute-start.56
  415.8 5.5 %collective-permute-done.55 = bf16[1,40,2176]{2,1,0:T(8,128)(2,1)S(1)} collective-permute-done((bf16[1,40,2176]{2,1,0:T(8,128)(2,1)S(1)}, bf16[1,40,2176]{2,1,0:T(8,128)(2,1)S(1)}, u32[]{:S(2)}, u32[]{:S(2)}) %collective-permute-start.55) | collective-permute-done | bytes 174112 | tf_op jit(solution)/shard_map/ppermute | solution.py:94
  421.3 3.6 collective-permute-done.56
  426.7 15.9 %collective-permute-done.59 = bf16[1,136,4352]{2,1,0:T(8,128)(2,1)S(1)} collective-permute-done((bf16[1,136,4352]{2,1,0:T(8,128)(2,1)}, bf16[1,136,4352]{2,1,0:T(8,128)(2,1)S(1)}, u32[]{:S(2)}, u32[]{:S(2)}) %collective-permute-start.59) | collective-permute-done | bytes 1183776 | tf_op jit(solution)/shard_map/ppermute | solution.py:94
  443.0 4.1 collective-permute-done.58
  449.0 2.6 bitcast_convert_fusion
  451.6 2.5 convert_element_type.367
  454.1 4.5 collective-permute-done.60
  (448 shorter events, 152.7 us)
Async XLA Ops:
  6.9 19.9 %collective-permute-start.5 = (bf16[1,8,272]{2,1,0:T(8,128)(2,1)}, bf16[1,8,272]{2,1,0:T(8,128)(2,1)}, u32[]{:S(2)}, u32[]{:S(2)}) collective-permute-start(bf16[1,8,272]{2,1,0:T(8,128)(2,1)} %bitcast.11), channel_id=1, source_target_pairs={{0,2},{1,3},{2,0},{3,1},{4,6},{5,7},{6,4},{7,5},{8,10},{9,11},{10,... | collective-permute-start | bytes 13064 | tf_op jit(solution)/shard_map/ppermute | solution.py:46
  11.5 84.3 %collective-permute-start.11 = (bf16[48,1088]{1,0:T(8,128)(2,1)}, bf16[48,1088]{1,0:T(8,128)(2,1)}, u32[]{:S(2)}, u32[]{:S(2)}) collective-permute-start(bf16[48,1088]{1,0:T(8,128)(2,1)} %get-tuple-element.273), channel_id=1, source_target_pairs={{1,0},{2,1},{3,2},{5,4},{6,5},{7,6},{9,8},{10,9},{11,10},{13,12},{... | collective-permute-start | bytes 313352 | tf_op jit(solution)/shard_map/ppermute | solution.py:540
  12.8 18.7 %collective-permute-start.3 = (bf16[256,1088]{0,1:T(8,128)(2,1)}, bf16[256,1088]{0,1:T(8,128)(2,1)}, u32[]{:S(2)}, u32[]{:S(2)}) collective-permute-start(bf16[256,1088]{0,1:T(8,128)(2,1)} %bitcast.126), channel_id=1, source_target_pairs={{0,2},{1,3},{2,0},{3,1},{4,6},{5,7},{6,4},{7,5},{8,10},{9,11},{10,... | collective-permute-start | bytes 1671176 | tf_op jit(solution)/shard_map/ppermute | solution.py:46
  21.8 32.4 %collective-permute-start.2 = (bf16[1,272,960]{2,1,0:T(8,128)(2,1)}, bf16[1,272,960]{2,1,0:T(8,128)(2,1)}, u32[]{:S(2)}, u32[]{:S(2)}) collective-permute-start(bf16[1,272,960]{2,1,0:T(8,128)(2,1)} %get-tuple-element.241), channel_id=1, source_target_pairs={{0,3},{1,2},{2,1},{3,0},{4,7},{5,6},{6,5},{7,4},{8,11},{9,10},{10,... | collective-permute-start | bytes 1566728 | tf_op jit(solution)/shard_map/ppermute | solution.py:46
  28.7 24.6 %collective-permute-start.1 = (bf16[1,272,960]{2,1,0:T(8,128)(2,1)}, bf16[1,272,960]{2,1,0:T(8,128)(2,1)S(1)}, u32[]{:S(2)}, u32[]{:S(2)}) collective-permute-start(bf16[1,272,960]{2,1,0:T(8,128)(2,1)} %get-tuple-element.242), channel_id=1, source_target_pairs={{0,2},{1,3},{2,0},{3,1},{4,6},{5,7},{6,4},{7,5},{8,10},{9,11},{10,... | collective-permute-start | bytes 1566728 | tf_op jit(solution)/shard_map/ppermute | solution.py:46
  33.7 41.2 %collective-permute-start.4 = (bf16[512,1088]{0,1:T(8,128)(2,1)}, bf16[512,1088]{0,1:T(8,128)(2,1)}, u32[]{:S(2)}, u32[]{:S(2)}) collective-permute-start(bf16[512,1088]{0,1:T(8,128)(2,1)} %pad_maximum_fusion.8), channel_id=1, source_target_pairs={{0,1},{1,0},{2,3},{3,2},{4,5},{5,4},{6,7},{7,6},{8,9},{9,8},{10,11... | collective-permute-start | bytes 3342344 | tf_op jit(solution)/shard_map/ppermute | solution.py:46
  57.2 17.7 %collective-permute-start.7 = (bf16[1,272,1088]{2,1,0:T(8,128)(2,1)}, bf16[1,272,1088]{2,1,0:T(8,128)(2,1)}, u32[]{:S(2)}, u32[]{:S(2)}) collective-permute-start(bf16[1,272,1088]{2,1,0:T(8,128)(2,1)} %get-tuple-element.233), channel_id=1, source_target_pairs={{0,1},{1,0},{2,3},{3,2},{4,5},{5,4},{6,7},{7,6},{8,9},{9,8},{10,11... | collective-permute-start | bytes 1775624 | tf_op jit(solution)/shard_map/ppermute | solution.py:46
  58.2 9.3 %collective-permute-start.9 = (bf16[1,136,1088]{2,1,0:T(8,128)(2,1)}, bf16[1,136,1088]{2,1,0:T(8,128)(2,1)S(1)}, u32[]{:S(2)}, u32[]{:S(2)}) collective-permute-start(bf16[1,136,1088]{2,1,0:T(8,128)(2,1)} %get-tuple-element.231), channel_id=1, source_target_pairs={{0,3},{1,2},{2,1},{3,0},{4,7},{5,6},{6,5},{7,4},{8,11},{9,10},{10,... | collective-permute-start | bytes 887816 | tf_op jit(solution)/shard_map/ppermute | solution.py:46
  58.2 16.7 %collective-permute-start.8 = (bf16[1,136,1088]{2,1,0:T(8,128)(2,1)}, bf16[1,136,1088]{2,1,0:T(8,128)(2,1)}, u32[]{:S(2)}, u32[]{:S(2)}) collective-permute-start(bf16[1,136,1088]{2,1,0:T(8,128)(2,1)} %get-tuple-element.232), channel_id=1, source_target_pairs={{0,2},{1,3},{2,0},{3,1},{4,6},{5,7},{6,4},{7,5},{8,10},{9,11},{10,... | collective-permute-start | bytes 887816 | tf_op jit(solution)/shard_map/ppermute | solution.py:46
  67.4 28.4 %collective-permute-start.10 = (bf16[48,1088]{1,0:T(8,128)(2,1)}, bf16[48,1088]{1,0:T(8,128)(2,1)S(1)}, u32[]{:S(2)}, u32[]{:S(2)}) collective-permute-start(bf16[48,1088]{1,0:T(8,128)(2,1)} %get-tuple-element.274), channel_id=1, source_target_pairs={{0,1},{1,2},{2,3},{4,5},{5,6},{6,7},{8,9},{9,10},{10,11},{12,13},{... | collective-permute-start | bytes 313352 | tf_op jit(solution)/shard_map/ppermute | solution.py:539
  101.2 15.6 %collective-permute-start.14 = (bf16[256,1088]{0,1:T(8,128)(2,1)}, bf16[256,1088]{0,1:T(8,128)(2,1)S(1)}, u32[]{:S(2)}, u32[]{:S(2)}) collective-permute-start(bf16[256,1088]{0,1:T(8,128)(2,1)} %bitcast_convert_fusion.1), channel_id=1, source_target_pairs={{0,2},{1,3},{2,0},{3,1},{4,6},{5,7},{6,4},{7,5},{8,10},{9,11},{10,... | collective-permute-start | bytes 1671176 | tf_op jit(solution)/shard_map/ppermute | solution.py:46
  105.4 23.0 %collective-permute-start.13 = (bf16[256,1088]{0,1:T(8,128)(2,1)S(1)}, bf16[256,1088]{0,1:T(8,128)(2,1)S(1)}, u32[]{:S(2)}, u32[]{:S(2)}) collective-permute-start(bf16[256,1088]{0,1:T(8,128)(2,1)S(1)} %slice.534), channel_id=1, source_target_pairs={{0,2},{1,3},{2,0},{3,1},{4,6},{5,7},{6,4},{7,5},{8,10},{9,11},{10,... | collective-permute-start | bytes 1671176 | tf_op jit(solution)/shard_map/ppermute | solution.py:46
  116.9 28.0 %collective-permute-start.15 = (bf16[512,1088]{0,1:T(8,128)(2,1)S(1)}, bf16[512,1088]{0,1:T(8,128)(2,1)S(1)}, u32[]{:S(2)}, u32[]{:S(2)}) collective-permute-start(bf16[512,1088]{0,1:T(8,128)(2,1)S(1)} %pad_maximum_fusion.9), channel_id=1, source_target_pairs={{0,1},{1,0},{2,3},{3,2},{4,5},{5,4},{6,7},{7,6},{8,9},{9,8},{10,11... | collective-permute-start | bytes 3342344 | tf_op jit(solution)/shard_map/ppermute | solution.py:46
  118.0 26.6 %collective-permute-start.18 = (bf16[2,136,1088]{2,1,0:T(8,128)(2,1)S(1)}, bf16[2,136,1088]{2,1,0:T(8,128)(2,1)S(1)}, u32[]{:S(2)}, u32[]{:S(2)}) collective-permute-start(bf16[2,136,1088]{2,1,0:T(8,128)(2,1)S(1)} %constant_dynamic-update-slice_fusion.13), channel_id=1, source_target_pairs={{0,4},{4,0},{8,12},{12,8},{16,20},{20,16},{24,28},{28,24},{1,5},{5... | collective-permute-start | bytes 1775624 | tf_op jit(solution)/shard_map/ppermute | solution.py:94
  130.1 14.3 %collective-permute-start.16 = (bf16[256,1088]{0,1:T(8,128)(2,1)S(1)}, bf16[256,1088]{0,1:T(8,128)(2,1)S(1)}, u32[]{:S(2)}, u32[]{:S(2)}) collective-permute-start(bf16[256,1088]{0,1:T(8,128)(2,1)S(1)} %add_convert_fusion.7), channel_id=1, source_target_pairs={{0,2},{1,3},{2,0},{3,1},{4,6},{5,7},{6,4},{7,5},{8,10},{9,11},{10,... | collective-permute-start | bytes 1671176 | tf_op jit(solution)/shard_map/ppermute | solution.py:46
  183.0 30.4 %collective-permute-start.24 = (bf16[1,544,1088]{2,1,0:T(8,128)(2,1)S(1)}, bf16[1,544,1088]{2,1,0:T(8,128)(2,1)S(1)}, u32[]{:S(2)}, u32[]{:S(2)}) collective-permute-start(bf16[1,544,1088]{2,1,0:T(8,128)(2,1)S(1)} %dynamic-slice_bitcast_fusion), channel_id=1, source_target_pairs={{0,4},{4,0},{8,12},{12,8},{16,20},{20,16},{24,28},{28,24},{1,5},{5... | collective-permute-start | bytes 3551240 | tf_op jit(solution)/shard_map/ppermute | solution.py:94
  186.3 27.1 %collective-permute-start.20 = (bf16[256,1088]{0,1:T(8,128)(2,1)S(1)}, bf16[256,1088]{0,1:T(8,128)(2,1)S(1)}, u32[]{:S(2)}, u32[]{:S(2)}) collective-permute-start(bf16[256,1088]{0,1:T(8,128)(2,1)S(1)} %slice.533), channel_id=1, source_target_pairs={{0,2},{1,3},{2,0},{3,1},{4,6},{5,7},{6,4},{7,5},{8,10},{9,11},{10,... | collective-permute-start | bytes 1671176 | tf_op jit(solution)/shard_map/ppermute | solution.py:46
  190.9 48.9 %collective-permute-start.23 = (bf16[4,136,1088]{2,1,0:T(8,128)(2,1)S(1)}, bf16[4,136,1088]{2,1,0:T(8,128)(2,1)S(1)}, u32[]{:S(2)}, u32[]{:S(2)}) collective-permute-start(bf16[4,136,1088]{2,1,0:T(8,128)(2,1)S(1)} %constant_dynamic-slice_fusion.20), channel_id=1, source_target_pairs={{0,4},{4,0},{8,12},{12,8},{16,20},{20,16},{24,28},{28,24},{1,5},{5... | collective-permute-start | bytes 3551240 | tf_op jit(solution)/shard_map/ppermute | solution.py:94
  215.7 13.5 %collective-permute-start.21 = (bf16[256,1088]{0,1:T(8,128)(2,1)S(1)}, bf16[256,1088]{0,1:T(8,128)(2,1)S(1)}, u32[]{:S(2)}, u32[]{:S(2)}) collective-permute-start(bf16[256,1088]{0,1:T(8,128)(2,1)S(1)} %get-tuple-element.225), channel_id=1, source_target_pairs={{0,2},{1,3},{2,0},{3,1},{4,6},{5,7},{6,4},{7,5},{8,10},{9,11},{10,... | collective-permute-start | bytes 1671176 | tf_op jit(solution)/shard_map/ppermute | solution.py:46
  216.7 17.4 %collective-permute-start.25 = (bf16[1,272,1088]{2,1,0:T(8,128)(2,1)S(1)}, bf16[1,272,1088]{2,1,0:T(8,128)(2,1)S(1)}, u32[]{:S(2)}, u32[]{:S(2)}) collective-permute-start(bf16[1,272,1088]{2,1,0:T(8,128)(2,1)S(1)} %constant_dynamic-slice_fusion.19), channel_id=1, source_target_pairs={{0,8},{4,12},{8,0},{12,4},{16,24},{20,28},{24,16},{28,20},{1,9},{5... | collective-permute-start | bytes 1775624 | tf_op jit(solution)/shard_map/ppermute | solution.py:94
  234.4 17.5 %collective-permute-start.26 = (bf16[1,136,1088]{2,1,0:T(8,128)(2,1)S(1)}, bf16[1,136,1088]{2,1,0:T(8,128)(2,1)S(1)}, u32[]{:S(2)}, u32[]{:S(2)}) collective-permute-start(bf16[1,136,1088]{2,1,0:T(8,128)(2,1)S(1)} %constant_dynamic-slice_fusion.18), channel_id=1, source_target_pairs={{0,16},{4,20},{8,24},{12,28},{16,0},{20,4},{24,8},{28,12},{1,17},{... | collective-permute-start | bytes 887816 | tf_op jit(solution)/shard_map/ppermute | solution.py:94
  252.6 46.2 %collective-permute-start.29 = (bf16[1,136,1088]{2,1,0:T(8,128)(2,1)}, bf16[1,136,1088]{2,1,0:T(8,128)(2,1)}, u32[]{:S(2)}, u32[]{:S(2)}) collective-permute-start(bf16[1,136,1088]{2,1,0:T(8,128)(2,1)} %add_convert_fusion.11), channel_id=1, source_target_pairs={{0,16},{4,20},{8,24},{12,28},{16,0},{20,4},{24,8},{28,12},{1,17},{... | collective-permute-start | bytes 887816 | tf_op jit(solution)/shard_map/ppermute | solution.py:94
  279.0 19.7 %collective-permute-start.30 = (bf16[4,72,1088]{2,1,0:T(8,128)(2,1)S(1)}, bf16[4,72,1088]{2,1,0:T(8,128)(2,1)S(1)}, u32[]{:S(2)}, u32[]{:S(2)}) collective-permute-start(bf16[4,72,1088]{2,1,0:T(8,128)(2,1)S(1)} %constant_dynamic-slice_fusion.17), channel_id=1, source_target_pairs={{0,8},{4,12},{8,0},{12,4},{16,24},{20,28},{24,16},{28,20},{1,9},{5... | collective-permute-start | bytes 1880072 | tf_op jit(solution)/shard_map/ppermute | solution.py:94
  283.9 55.5 %collective-permute-start.34 = (bf16[4,136,544]{2,1,0:T(8,128)(2,1)}, bf16[4,136,544]{2,1,0:T(8,128)(2,1)}, u32[]{:S(2)}, u32[]{:S(2)}) collective-permute-start(bf16[4,136,544]{2,1,0:T(8,128)(2,1)} %constant_dynamic-slice_fusion.13), channel_id=1, source_target_pairs={{0,4},{4,0},{8,12},{12,8},{16,20},{20,16},{24,28},{28,24},{1,5},{5... | collective-permute-start | bytes 1775624 | tf_op jit(solution)/shard_map/ppermute | solution.py:94
  287.0 52.9 %collective-permute-start.35 = (bf16[4,136,544]{2,1,0:T(8,128)(2,1)S(1)}, bf16[4,136,544]{2,1,0:T(8,128)(2,1)}, u32[]{:S(2)}, u32[]{:S(2)}) collective-permute-start(bf16[4,136,544]{2,1,0:T(8,128)(2,1)S(1)} %constant_dynamic-slice_fusion.12), channel_id=1, source_target_pairs={{0,8},{4,12},{8,0},{12,4},{16,24},{20,28},{24,16},{28,20},{1,9},{5... | collective-permute-start | bytes 1775624 | tf_op jit(solution)/shard_map/ppermute | solution.py:94
  290.7 13.1 %collective-permute-start.27 = (bf16[512,1088]{0,1:T(8,128)(2,1)S(1)}, bf16[512,1088]{0,1:T(8,128)(2,1)S(1)}, u32[]{:S(2)}, u32[]{:S(2)}) collective-permute-start(bf16[512,1088]{0,1:T(8,128)(2,1)S(1)} %slice.528), channel_id=1, source_target_pairs={{0,1},{1,0},{2,3},{3,2},{4,5},{5,4},{6,7},{7,6},{8,9},{9,8},{10,11... | collective-permute-start | bytes 3342344 | tf_op jit(solution)/shard_map/ppermute | solution.py:46
  298.9 22.1 %collective-permute-start.32 = (bf16[4,40,1088]{2,1,0:T(8,128)(2,1)S(1)}, bf16[4,40,1088]{2,1,0:T(8,128)(2,1)S(1)}, u32[]{:S(2)}, u32[]{:S(2)}) collective-permute-start(bf16[4,40,1088]{2,1,0:T(8,128)(2,1)S(1)} %constant_dynamic-slice_fusion.15), channel_id=1, source_target_pairs={{0,16},{4,20},{8,24},{12,28},{16,0},{20,4},{24,8},{28,12},{1,17},{... | collective-permute-start | bytes 1044488 | tf_op jit(solution)/shard_map/ppermute | solution.py:94
  301.9 32.3 %collective-permute-start.36 = (bf16[1,272,1088]{2,1,0:T(8,128)(2,1)S(1)}, bf16[1,272,1088]{2,1,0:T(8,128)(2,1)S(1)}, u32[]{:S(2)}, u32[]{:S(2)}) collective-permute-start(bf16[1,272,1088]{2,1,0:T(8,128)(2,1)S(1)} %pad_maximum_fusion.15), channel_id=1, source_target_pairs={{0,8},{4,12},{8,0},{12,4},{16,24},{20,28},{24,16},{28,20},{1,9},{5... | collective-permute-start | bytes 1775624 | tf_op jit(solution)/shard_map/ppermute | solution.py:94
  321.2 14.2 %collective-permute-start.39 = (bf16[1,40,1088]{2,1,0:T(8,128)(2,1)S(1)}, bf16[1,40,1088]{2,1,0:T(8,128)(2,1)S(1)}, u32[]{:S(2)}, u32[]{:S(2)}) collective-permute-start(bf16[1,40,1088]{2,1,0:T(8,128)(2,1)S(1)} %get-tuple-element.280), channel_id=1, source_target_pairs={{0,3},{1,2},{2,1},{3,0},{4,7},{5,6},{6,5},{7,4},{8,11},{9,10},{10,... | collective-permute-start | bytes 261128 | tf_op jit(solution)/shard_map/ppermute | solution.py:46
  321.3 14.2 %collective-permute-start.38 = (bf16[1,40,1088]{2,1,0:T(8,128)(2,1)S(1)}, bf16[1,40,1088]{2,1,0:T(8,128)(2,1)S(1)}, u32[]{:S(2)}, u32[]{:S(2)}) collective-permute-start(bf16[1,40,1088]{2,1,0:T(8,128)(2,1)S(1)} %get-tuple-element.281), channel_id=1, source_target_pairs={{0,2},{1,3},{2,0},{3,1},{4,6},{5,7},{6,4},{7,5},{8,10},{9,11},{10,... | collective-permute-start | bytes 261128 | tf_op jit(solution)/shard_map/ppermute | solution.py:46
  335.4 15.7 %collective-permute-start.33 = (bf16[256,1088]{0,1:T(8,128)(2,1)}, bf16[256,1088]{0,1:T(8,128)(2,1)}, u32[]{:S(2)}, u32[]{:S(2)}) collective-permute-start(bf16[256,1088]{0,1:T(8,128)(2,1)} %slice.531), channel_id=1, source_target_pairs={{0,2},{1,3},{2,0},{3,1},{4,6},{5,7},{6,4},{7,5},{8,10},{9,11},{10,... | collective-permute-start | bytes 1671176 | tf_op jit(solution)/shard_map/ppermute | solution.py:46
  335.5 27.3 %collective-permute-start.31 = (bf16[256,1088]{0,1:T(8,128)(2,1)}, bf16[256,1088]{0,1:T(8,128)(2,1)}, u32[]{:S(2)}, u32[]{:S(2)}) collective-permute-start(bf16[256,1088]{0,1:T(8,128)(2,1)} %slice.532), channel_id=1, source_target_pairs={{0,2},{1,3},{2,0},{3,1},{4,6},{5,7},{6,4},{7,5},{8,10},{9,11},{10,... | collective-permute-start | bytes 1671176 | tf_op jit(solution)/shard_map/ppermute | solution.py:46
  337.5 65.5 %collective-permute-start.50 = (bf16[1,544,1088]{2,1,0:T(8,128)(2,1)}, bf16[1,544,1088]{2,1,0:T(8,128)(2,1)}, u32[]{:S(2)}, u32[]{:S(2)}) collective-permute-start(bf16[1,544,1088]{2,1,0:T(8,128)(2,1)} %pad_maximum_fusion.6), channel_id=1, source_target_pairs={{0,4},{4,0},{8,12},{12,8},{16,20},{20,16},{24,28},{28,24},{1,5},{5... | collective-permute-start | bytes 3551240 | tf_op jit(solution)/shard_map/ppermute | solution.py:94
  339.4 31.6 %collective-permute-start.42 = (bf16[1,40,4352]{2,1,0:T(8,128)(2,1)S(1)}, bf16[1,40,4352]{2,1,0:T(8,128)(2,1)S(1)}, u32[]{:S(2)}, u32[]{:S(2)}) collective-permute-start(bf16[1,40,4352]{2,1,0:T(8,128)(2,1)S(1)} %bitcast.134), channel_id=1, source_target_pairs={{0,16},{4,20},{8,24},{12,28},{16,0},{20,4},{24,8},{28,12},{1,17},{... | collective-permute-start | bytes 1044488 | tf_op jit(solution)/shard_map/ppermute | solution.py:94
  342.2 33.1 %collective-permute-start.41 = (bf16[4,72,544]{2,1,0:T(8,128)(2,1)}, bf16[4,72,544]{2,1,0:T(8,128)(2,1)}, u32[]{:S(2)}, u32[]{:S(2)}) collective-permute-start(bf16[4,72,544]{2,1,0:T(8,128)(2,1)} %constant_dynamic-slice_fusion.6), channel_id=1, source_target_pairs={{0,4},{4,0},{8,12},{12,8},{16,20},{20,16},{24,28},{28,24},{1,5},{5... | collective-permute-start | bytes 940040 | tf_op jit(solution)/shard_map/ppermute | solution.py:94
  351.2 24.1 %collective-permute-start.40 = (bf16[4,72,544]{2,1,0:T(8,128)(2,1)}, bf16[4,72,544]{2,1,0:T(8,128)(2,1)}, u32[]{:S(2)}, u32[]{:S(2)}) collective-permute-start(bf16[4,72,544]{2,1,0:T(8,128)(2,1)} %constant_dynamic-slice_fusion.7), channel_id=1, source_target_pairs={{0,8},{4,12},{8,0},{12,4},{16,24},{20,28},{24,16},{28,20},{1,9},{5... | collective-permute-start | bytes 940040 | tf_op jit(solution)/shard_map/ppermute | solution.py:94
  379.5 20.3 %collective-permute-start.46 = (bf16[4,40,544]{2,1,0:T(8,128)(2,1)S(1)}, bf16[4,40,544]{2,1,0:T(8,128)(2,1)S(1)}, u32[]{:S(2)}, u32[]{:S(2)}) collective-permute-start(bf16[4,40,544]{2,1,0:T(8,128)(2,1)S(1)} %constant_dynamic-slice_fusion), channel_id=1, source_target_pairs={{0,16},{4,20},{8,24},{12,28},{16,0},{20,4},{24,8},{28,12},{1,17},{... | collective-permute-start | bytes 522248 | tf_op jit(solution)/shard_map/ppermute | solution.py:94
  380.0 19.8 %collective-permute-start.45 = (bf16[4,40,544]{2,1,0:T(8,128)(2,1)S(1)}, bf16[4,40,544]{2,1,0:T(8,128)(2,1)S(1)}, u32[]{:S(2)}, u32[]{:S(2)}) collective-permute-start(bf16[4,40,544]{2,1,0:T(8,128)(2,1)S(1)} %constant_dynamic-slice_fusion.1), channel_id=1, source_target_pairs={{0,16},{4,20},{8,24},{12,28},{16,0},{20,4},{24,8},{28,12},{1,17},{... | collective-permute-start | bytes 522248 | tf_op jit(solution)/shard_map/ppermute | solution.py:94
  382.5 17.3 %collective-permute-start.49 = (f32[3264]{0:T(1024)S(1)}, f32[3264]{0:T(1024)S(1)}, u32[]{:S(2)}, u32[]{:S(2)}) collective-permute-start(f32[3264]{0:T(1024)S(1)} %add.436), channel_id=1, source_target_pairs={{0,16},{4,20},{8,24},{12,28},{16,0},{20,4},{24,8},{28,12},{1,17},{... | collective-permute-start | bytes 39176 | tf_op jit(solution)/shard_map/ppermute | solution.py:94
  385.2 22.8 %collective-permute-start.54 = (bf16[1,72,4352]{2,1,0:T(8,128)(2,1)S(1)}, bf16[1,72,4352]{2,1,0:T(8,128)(2,1)S(1)}, u32[]{:S(2)}, u32[]{:S(2)}) collective-permute-start(bf16[1,72,4352]{2,1,0:T(8,128)(2,1)S(1)} %pad_maximum_fusion.16), channel_id=1, source_target_pairs={{0,8},{4,12},{8,0},{12,4},{16,24},{20,28},{24,16},{28,20},{1,9},{5... | collective-permute-start | bytes 1880072 | tf_op jit(solution)/shard_map/ppermute | solution.py:94
  400.7 8.7 %collective-permute-start.53 = (bf16[1,40,816]{2,1,0:T(8,128)(2,1)S(1)}, bf16[1,40,816]{2,1,0:T(8,128)(2,1)S(1)}, u32[]{:S(2)}, u32[]{:S(2)}) collective-permute-start(bf16[1,40,816]{2,1,0:T(8,128)(2,1)S(1)} %get-tuple-element.284), channel_id=1, source_target_pairs={{0,3},{1,2},{2,1},{3,0},{4,7},{5,6},{6,5},{7,4},{8,11},{9,10},{10,... | collective-permute-start | bytes 195848 | tf_op jit(solution)/shard_map/ppermute | solution.py:46
  410.1 11.2 %collective-permute-start.55 = (bf16[1,40,2176]{2,1,0:T(8,128)(2,1)S(1)}, bf16[1,40,2176]{2,1,0:T(8,128)(2,1)S(1)}, u32[]{:S(2)}, u32[]{:S(2)}) collective-permute-start(bf16[1,40,2176]{2,1,0:T(8,128)(2,1)S(1)} %bitcast.146), channel_id=1, source_target_pairs={{0,16},{4,20},{8,24},{12,28},{16,0},{20,4},{24,8},{28,12},{1,17},{... | collective-permute-start | bytes 522248 | tf_op jit(solution)/shard_map/ppermute | solution.py:94
  410.6 14.3 %collective-permute-start.56 = (bf16[1,40,2176]{2,1,0:T(8,128)(2,1)S(1)}, bf16[1,40,2176]{2,1,0:T(8,128)(2,1)S(1)}, u32[]{:S(2)}, u32[]{:S(2)}) collective-permute-start(bf16[1,40,2176]{2,1,0:T(8,128)(2,1)S(1)} %bitcast.148), channel_id=1, source_target_pairs={{0,16},{4,20},{8,24},{12,28},{16,0},{20,4},{24,8},{28,12},{1,17},{... | collective-permute-start | bytes 522248 | tf_op jit(solution)/shard_map/ppermute | solution.py:94
  414.2 28.4 %collective-permute-start.59 = (bf16[1,136,4352]{2,1,0:T(8,128)(2,1)}, bf16[1,136,4352]{2,1,0:T(8,128)(2,1)S(1)}, u32[]{:S(2)}, u32[]{:S(2)}) collective-permute-start(bf16[1,136,4352]{2,1,0:T(8,128)(2,1)} %pad_maximum_fusion.7), channel_id=1, source_target_pairs={{0,4},{4,0},{8,12},{12,8},{16,20},{20,16},{24,28},{28,24},{1,5},{5... | collective-permute-start | bytes 3551240 | tf_op jit(solution)/shard_map/ppermute | solution.py:94
  425.0 22.1 %collective-permute-start.58 = (bf16[1,72,2176]{2,1,0:T(8,128)(2,1)S(1)}, bf16[1,72,2176]{2,1,0:T(8,128)(2,1)S(1)}, u32[]{:S(2)}, u32[]{:S(2)}) collective-permute-start(bf16[1,72,2176]{2,1,0:T(8,128)(2,1)S(1)} %pad_maximum_fusion.20), channel_id=1, source_target_pairs={{0,4},{4,0},{8,12},{12,8},{16,20},{20,16},{24,28},{28,24},{1,5},{5... | collective-permute-start | bytes 940040 | tf_op jit(solution)/shard_map/ppermute | solution.py:94
  426.6 20.5 %collective-permute-start.57 = (bf16[1,72,2176]{2,1,0:T(8,128)(2,1)S(1)}, bf16[1,72,2176]{2,1,0:T(8,128)(2,1)S(1)}, u32[]{:S(2)}, u32[]{:S(2)}) collective-permute-start(bf16[1,72,2176]{2,1,0:T(8,128)(2,1)S(1)} %pad_maximum_fusion.19), channel_id=1, source_target_pairs={{0,8},{4,12},{8,0},{12,4},{16,24},{20,28},{24,16},{28,20},{1,9},{5... | collective-permute-start | bytes 940040 | tf_op jit(solution)/shard_map/ppermute | solution.py:94
  447.3 11.4 %collective-permute-start.60 = (bf16[1,136,2176]{2,1,0:T(8,128)(2,1)S(1)}, bf16[1,136,2176]{2,1,0:T(8,128)(2,1)S(1)}, u32[]{:S(2)}, u32[]{:S(2)}) collective-permute-start(bf16[1,136,2176]{2,1,0:T(8,128)(2,1)S(1)} %pad_maximum_fusion.17), channel_id=1, source_target_pairs={{0,4},{4,0},{8,12},{12,8},{16,20},{20,16},{24,28},{28,24},{1,5},{5... | collective-permute-start | bytes 1775624 | tf_op jit(solution)/shard_map/ppermute | solution.py:94
  448.9 10.0 %collective-permute-start.61 = (bf16[1,136,2176]{2,1,0:T(8,128)(2,1)S(1)}, bf16[1,136,2176]{2,1,0:T(8,128)(2,1)S(1)}, u32[]{:S(2)}, u32[]{:S(2)}) collective-permute-start(bf16[1,136,2176]{2,1,0:T(8,128)(2,1)S(1)} %pad_maximum_fusion.18), channel_id=1, source_target_pairs={{0,8},{4,12},{8,0},{12,4},{16,24},{20,28},{24,16},{28,20},{1,9},{5... | collective-permute-start | bytes 1775624 | tf_op jit(solution)/shard_map/ppermute | solution.py:94
  (87 other events, 777.3 us)
